TPU v7x, 32 devices: a whole 2x2x4 slice. The times are simulated.
32 devices in a mesh: leaf: 8 (over z, y), front: 4 (over x, core).
Axes of the slice: x: 2, y: 2, z: 4, core: 2. Of those that a mesh axis runs over, the one named last changes fastest.
Arguments:
- leaf_fronts: float32 [8, 1, 2048, 2048], P('leaf', None, 'front'), may hold values from -40 to 40, as said below
- screen_weights: float32 [8, 1, 2048], P('leaf', None, 'front'), may hold values from 0.1 to 2
- parent_tile_index: int32 [8, 1, 12], replicated, may hold values from 0 to 31, as said below
Outputs:
- leaf_panel: float32 [8, 1, 2048, 512], P('leaf', None, 'front')
- parent_panel: float32 [8, 1, 2048, 128], P('leaf', None, 'front')
- parent_update: float32 [8, 1, 2048, 3968], P('leaf', None, 'front')
Inputs may be any that keep to these rules, and one draw needn't show every extreme that they name: `leaf_fronts`: each first-level front is symmetric positive definite. `parent_tile_index`: entry [i, g, a] is the tile of parent (i // 2, g) that receives contribution tile t = 4 * (a // 3) + a % 3 + 1 of front (i, g); tile p covers rows p * 128 to (p + 1) * 128 - 1. The entries of one front are distinct, tile 1 always goes to parent tile 0, and p * 128 // 1024 == t * 128 // 512.
All inputs are finite; a program needn't handle non-finite values.
Results may differ from a plain program's by a relative error of at most 0.00013.
Values sent between devices are 32-bit elements; how exact they have to be, the bound alone decides.
No kernel may reach another device: no remote copies, remote signals or barrier semaphores. Data moves between devices by JAX's collectives and lax.ppermute only.
A program may use at most 128 MiB of HBM per device.

v0:
```python
import functools

import jax
import jax.numpy as jnp
from jax import lax
from jax.experimental import pallas as pl
from jax.experimental.pallas import tpu as pltpu
from jax.sharding import PartitionSpec as P

SEP2 = 1024
PANEL_WIDTH = 128
M2 = 4096
GROUP_TILES = 4
SLAB = 8
EXACT = lax.Precision.HIGHEST
VMEM_BYTES = 60 * 2**20

TILE = PANEL_WIDTH
LAST = ((1,), (1,))
PLAIN = ((1,), (0,))


def from_front(value, distance):
    pairs = [(source, source ^ distance) for source in range(lax.axis_size("front"))]
    return lax.ppermute(value, "front", pairs)


def from_sibling(value):
    pairs = [(source, source ^ 1) for source in range(lax.axis_size("leaf"))]
    return lax.ppermute(value, "leaf", pairs)


def after(value, *events):
    return lax.optimization_barrier((value, *events))[0]


def slot_of(offset, count):
    slot, bit, weight = 0, 1, count // 2
    while weight:
        slot = slot + jnp.where((offset & bit) != 0, weight, 0)
        bit, weight = bit * 2, weight // 2
    return slot


def offset_of(slot, count):
    offset, bit, weight = 0, 1, count // 2
    while weight:
        offset += bit if slot & weight else 0
        bit, weight = bit * 2, weight // 2
    return offset


def exact_dot(left, right, contract):
    return lax.dot_general(
        left, right, (contract, ((), ())), precision=EXACT, preferred_element_type=jnp.float32
    )


def plain_dot(left, right):
    return lax.dot_general(left, right, (LAST, ((), ())), preferred_element_type=jnp.float32)


def halves(value):
    high = value.astype(jnp.bfloat16)
    return high, (value - high.astype(jnp.float32)).astype(jnp.bfloat16)


def split_dot(left, right):
    return plain_dot(left[0], right[0]) + (plain_dot(left[0], right[1]) + plain_dot(left[1], right[0]))


def lane(row, index):
    return jnp.broadcast_to(row[:, index : index + 1], row.shape)


def sum_tree(terms):
    while len(terms) > 1:
        terms = [sum(terms[i : i + 2]) for i in range(0, len(terms), 2)]
    return terms[0]


def factor_slab(block, first, inside, lanes):
    rows = [jnp.broadcast_to(block[i : i + 1, :], block.shape) for i in range(SLAB)]
    entry = {(i, j): lane(rows[i], first + j) for i in range(SLAB) for j in range(i + 1)}
    rows = [
        jnp.where(inside, jnp.where(lanes == first + i, 1.0, 0.0), row) for i, row in enumerate(rows)
    ]
    done = []
    for p in range(0, SLAB, 2):
        r = p + 1
        one, mixed, two = entry[p, p], entry[r, p], entry[r, r]
        inverse_one = pl.reciprocal(one, approx=True)
        inverse_two = pl.reciprocal(one * two - mixed * mixed, approx=True) * one
        factor = {i: entry[i, p] * inverse_one for i in range(r, SLAB)}
        rows[r] = rows[r] - factor[r] * rows[p]
        for i in range(p + 2, SLAB):
            entry[i, r] = entry[i, r] - factor[i] * mixed
        for i in range(p + 2, SLAB):
            second = entry[i, r] * inverse_two
            for k in range(p + 2, i + 1):
                entry[i, k] = (entry[i, k] - factor[i] * entry[k, p]) - second * entry[k, r]
            rows[i] = (rows[i] - factor[i] * rows[p]) - second * rows[r]
        done.append(rows[p] * lax.rsqrt(one))
        done.append(rows[r] * (inverse_two * lax.rsqrt(inverse_two)))
    return done


def factor_steps(a, fronts):
    sublanes = lax.broadcasted_iota(jnp.int32, (SLAB, TILE), 0)
    lanes = lax.broadcasted_iota(jnp.int32, (SLAB, TILE), 1)
    for start in range(0, TILE, SLAB):
        inside = (lanes >= start) & (lanes < start + SLAB)
        for q in range(fronts):
            rows = factor_slab(a[q, start : start + SLAB, :], start, inside, lanes)
            for low in range(start + SLAB, TILE, SLAB):
                chosen = sublanes + low
                terms = [jnp.take_along_axis(row, chosen, axis=1) * row for row in rows]
                block = a[q, low : low + SLAB, :]
                a[q, low : low + SLAB, :] = jnp.where(inside, 0.0, block) - sum_tree(terms)
            block = rows[0]
            for i in range(1, SLAB):
                block = jnp.where(sublanes == i, rows[i], block)
            a[q, start : start + SLAB, :] = block
        yield


def place():
    leaf, front = lax.axis_index("leaf"), lax.axis_index("front")
    return leaf, front, leaf & 1


def corner_kernel(*refs, order, first, last, count, devices):
    tiles = order // TILE
    if first == 0:
        near, other, work, out, heads, a = refs
    else:
        old_work, old_out, out, work, a = refs
    fronts = out.shape[0]
    if first == 0:
        front = place()[1]
        pieces = devices // 2

        def copy(owner, q, take):
            slot = slot_of(front ^ owner, devices)
            for held, low in ((near, 0), (other, pieces)):

                @pl.when((slot >= low) & (slot < low + pieces))
                def _():
                    take(held.at[q * pieces + slot - low])

        for q in range(fronts):
            for e in range(tiles):

                def take_tile(slab):
                    work[q, e * TILE : (e + 1) * TILE, :] = slab[:TILE, :]

                copy(e * GROUP_TILES // count, q, take_tile)

            def take_head(slab):
                heads[q] = slab[TILE:, :]

            copy(0, q, take_head)
    else:
        work[...] = old_work[...]
        out[...] = old_out[...]

    def step(k, carry):
        block = pl.ds(pl.multiple_of(k * TILE, TILE), TILE)
        for q in range(fronts):
            a[q] = work[q, block, block]
        for _ in factor_steps(a, fronts):
            pass
        kept = lax.broadcasted_iota(jnp.int32, (TILE, TILE), 0) >= lax.broadcasted_iota(jnp.int32, (TILE, TILE), 1)
        for q in range(fronts):
            out[q, block, block] = jnp.where(kept, a[q], 0.0)
        for fixed in range(first, last):

            @pl.when(k == fixed)
            def _():
                here = slice(fixed * TILE, (fixed + 1) * TILE)
                low, rest = slice(0, fixed * TILE), slice((fixed + 1) * TILE, order)
                for q in range(fronts):
                    corner = out[q, here, here]
                    if fixed:
                        chain = exact_dot(work[q, here, low], out[q, low, low], PLAIN)
                        out[q, here, low] = -exact_dot(corner, chain, PLAIN)
                    if fixed + 1 < tiles:
                        out[q, here, rest] = jnp.zeros((TILE, order - (fixed + 1) * TILE), jnp.float32)
                        below = exact_dot(work[q, rest, here], corner, LAST)
                        work[q, rest, here] = below
                        work[q, rest, rest] = work[q, rest, rest] - exact_dot(below, below, LAST)

        return carry

    lax.fori_loop(first, last, step, 0)


def parent_kernel(*refs, count, skip, width, devices):
    pieces = 2 * devices
    table, heads, weights, slab, inverse, fronts_here, far = refs[:7]
    edges = refs[7 : 7 + pieces]
    leaf_out, panel_out, update_out = refs[7 + pieces : 10 + pieces]
    (
        edge, here, beyond, leaf_panel, own_panel, panel_high, panel_low, column,
        two_left, two_right, total, a, edge_done, rows_done, out_done,
    ) = refs[10 + pieces :]
    leaf, front, half = place()
    sent = count - skip
    separator = width // GROUP_TILES
    rows = count * TILE
    first_row = pl.multiple_of((front * 2 + half) * rows, TILE)

    def at(tile):
        return pl.ds(pl.multiple_of(tile * TILE, TILE), TILE)

    def goal_of(i, tile):
        entry = 3 * (tile >> 2) + (tile & 3) - 1
        return jnp.where((tile & 3) == 0, -1, table[leaf ^ i, jnp.maximum(entry, 0)])

    copies = [
        pltpu.make_async_copy(edges[k], edge.at[k // devices, k % devices], edge_done.at[k]) for k in range(pieces)
    ]
    copies += [
        pltpu.make_async_copy(fronts_here.at[skip * TILE :, :], here, rows_done.at[0]),
        pltpu.make_async_copy(far, beyond, rows_done.at[1]),
    ]
    for copy in copies:
        copy.start()

    total[...] = jnp.zeros_like(total)
    column[...] = jnp.zeros_like(column)
    row_ids = lax.broadcasted_iota(jnp.int32, (TILE, TILE), 0)
    col_ids = lax.broadcasted_iota(jnp.int32, (TILE, TILE), 1)
    near = jnp.where(jnp.abs(row_ids - col_ids) == 1, 1.0, 0.0)
    before = jnp.where((row_ids == 0) & (col_ids == TILE - 1), 1.0, 0.0)
    behind = jnp.where((row_ids == TILE - 1) & (col_ids == 0), 1.0, 0.0)
    first_weights = jnp.where(half == 0, heads[0, 0:1, :TILE], heads[1, 0:1, :TILE])
    column[:TILE, :] = jnp.where(row_ids == col_ids, first_weights + 4.0, 0.0) - near
    column[TILE : 2 * TILE, :] = -before
    inside = first_row < SEP2
    weight = jnp.transpose(jnp.broadcast_to(weights[...], (TILE, rows)))
    for j in range(count):
        mine = (front * 2 + half) * count + j
        line = slice(j * TILE, (j + 1) * TILE)
        total[line, at(mine)] = jnp.where(
            row_ids == col_ids, weight[line, :] + jnp.where(inside, 4.0, 0.0), 0.0
        ) - jnp.where(inside, near, 0.0)

        @pl.when((mine > 0) & inside)
        def _():
            total[line, at(mine - 1)] = -before

        @pl.when((mine + 1) * TILE < SEP2)
        def _():
            total[line, at(mine + 1)] = -behind

    leaf_copy = pltpu.make_async_copy(leaf_panel, leaf_out, out_done.at[0])
    for i in range(2):
        turned = halves(inverse[i])
        cut = separator // 2
        top = tuple(part[:cut, :cut] for part in turned)
        bottom = tuple(part[cut:, :] for part in turned)

        def panel_of(block):
            full = halves(block)
            return jnp.concatenate(
                [split_dot(tuple(part[:, :cut] for part in full), top), split_dot(full, bottom)], axis=1
            )

        for s in range(devices):
            copies[i * devices + s].wait()
            panel = panel_of(edge[i, s, :, :separator])
            if s == 0 and i == 0:
                leaf_panel[skip * TILE :, :] = panel
                if skip:
                    leaf_panel[:TILE, :] = panel_of(slab[:TILE, :])
                leaf_copy.start()
            panel_high[i, s], panel_low[i, s] = halves(panel)

    tile_one = slice((1 - skip) * TILE, (2 - skip) * TILE)
    slot = slot_of(front, devices)
    for i in range(2):
        one = panel_high[i, slot, tile_one, :], panel_low[i, slot, tile_one, :]
        for s in range(devices):
            piece = edge[i, s, :, separator:] - split_dot((panel_high[i, s], panel_low[i, s]), one)
            owner = front ^ offset_of(s, devices)
            for t in range(sent):
                target = goal_of(i, owner * count + skip + t)

                @pl.when(target >= 0)
                def _():
                    column[at(target), :] += piece[t * TILE : (t + 1) * TILE, :]

    copies[-2].wait()
    copies[-1].wait()

    def contribution(i, s):
        product = split_dot((panel_high[i, 0], panel_low[i, 0]), (panel_high[i, s], panel_low[i, s]))
        for c in range(sent):
            tile = (front ^ offset_of(s, devices)) * count + skip + c
            goal = jnp.maximum(goal_of(i, tile), 0)
            for t in range(sent):
                target = goal_of(i, front * count + skip + t) - (front * 2 + half) * count
                target = jnp.where((target >= 0) & (target < count), target, count)
                line = slice(t * TILE, (t + 1) * TILE)
                if i == 0:
                    source = here[line, at(tile)]
                else:
                    source = beyond[line, at(jnp.maximum(tile - (tile >> 2) - 2, 0))]
                total[at(target), at(goal)] += source - product[line, c * TILE : (c + 1) * TILE]

    work = [functools.partial(contribution, i, s) for i in range(2) for s in range(devices)]
    a[0] = column[:TILE, :]
    steps = TILE // SLAB
    for k, _ in enumerate(factor_steps(a, 1)):
        while work and len(work) * steps >= (steps - k) * (2 * devices):
            work.pop(0)()
    for task in work:
        task()

    turned = halves(jnp.where(row_ids >= col_ids, a[0], 0.0))
    for start in range(0, M2, 1024):
        block = slice(start, start + 1024)
        panel = split_dot(halves(column[block, :]), turned)
        column[block, :] = panel
        high, low = halves(panel)
        two_left[block, :] = jnp.concatenate([high, high, low], axis=1)
        two_right[block, :] = jnp.concatenate([high, low, high], axis=1)
    mine = pl.ds(first_row, rows)
    own_panel[...] = column[mine, :]
    panel_copy = pltpu.make_async_copy(own_panel, panel_out, out_done.at[1])
    panel_copy.start()
    own = two_left[mine, :]
    sends = [leaf_copy, panel_copy]
    for start in range(TILE, M2, 512):
        stop = min(start + 512, M2)
        total[:rows, start:stop] = total[:rows, start:stop] - plain_dot(own, two_right[start:stop, :])
        send = pltpu.make_async_copy(
            total.at[:rows, start:stop],
            update_out.at[:, start - TILE : stop - TILE],
            out_done.at[len(sends)],
        )
        send.start()
        sends.append(send)
    for send in sends:
        send.wait()


def one_front(matrix, weights, table):
    rows, width = matrix.shape
    devices = lax.axis_size("front")
    count, tiles = rows // TILE, width // TILE
    skip = 1 if count % GROUP_TILES == 0 else 0
    separator = width // GROUP_TILES
    sent = (count - skip) * TILE
    distances = []
    while 2 ** (len(distances) + 1) < devices:
        distances.insert(0, 2 ** (len(distances) + 1))

    def columns(block, chosen):
        return jnp.concatenate([block[:, t * TILE : (t + 1) * TILE] for t in chosen], axis=1)

    def spread(pieces):
        for distance in distances:
            pieces = pieces + [from_front(piece, distance) for piece in pieces]
        return pieces

    corner = list(range(0, tiles, GROUP_TILES))
    rest = [t for t in range(tiles) if t % GROUP_TILES and t != 1]
    weight_rows = jnp.pad(weights[None], ((0, SLAB - 1), (0, separator - rows)))
    slab = jnp.concatenate([columns(matrix[:TILE], corner), weight_rows], axis=0)
    body = matrix[skip * TILE :]
    far_slab = from_sibling(slab)
    slabs = spread([slab])
    edge = columns(body, corner + [1])
    far_body = columns(body, rest)
    far_slabs = spread([far_slab])
    held = jnp.stack(slabs + far_slabs)
    other = from_front(held, 1)
    far_edge = from_sibling(after(edge, far_slab))
    far = from_sibling(after(far_body, far_slab))
    near_edges = spread([after(edge, *far_slabs)])

    vmem = pl.BlockSpec(memory_space=pltpu.VMEM)
    smem = pl.BlockSpec(memory_space=pltpu.SMEM)
    anywhere = pl.BlockSpec(memory_space=pl.ANY)
    f32, bf16 = jnp.float32, jnp.bfloat16
    state = jax.ShapeDtypeStruct((2, separator, separator), f32)
    scratch = pltpu.VMEM((2, TILE, TILE), f32)
    params = pltpu.CompilerParams(vmem_limit_bytes=VMEM_BYTES)
    cost = pl.CostEstimate(flops=12 * 10**9, bytes_accessed=2**23, transcendentals=0)
    middle = separator // TILE // 2
    half_kernel = functools.partial(corner_kernel, order=separator, count=count, devices=devices)
    state_one, state_two, heads = pl.pallas_call(
        functools.partial(half_kernel, first=0, last=middle),
        out_shape=(state, state, jax.ShapeDtypeStruct((2, SLAB, separator), f32)),
        in_specs=[vmem, vmem],
        out_specs=(vmem, vmem, vmem),
        scratch_shapes=[scratch],
        compiler_params=params,
        cost_estimate=cost,
        name="corner_first",
    )(held, other)

    other_edges = [from_front(after(piece, heads), 1) for piece in near_edges]
    far_edges = spread([after(far_edge, heads)])
    inverse = pl.pallas_call(
        functools.partial(half_kernel, first=middle, last=separator // TILE),
        out_shape=state,
        in_specs=[vmem, vmem],
        out_specs=vmem,
        scratch_shapes=[pltpu.VMEM((2, separator, separator), f32), scratch],
        compiler_params=params,
        cost_estimate=cost,
        name="corner_second",
    )(after(state_one, far_edge), state_two)
    other_far_edges = [from_front(piece, 1) for piece in far_edges]

    edges = near_edges + other_edges + far_edges + other_far_edges
    return pl.pallas_call(
        functools.partial(parent_kernel, count=count, skip=skip, width=width, devices=devices),
        out_shape=(
            jax.ShapeDtypeStruct((rows, separator), f32),
            jax.ShapeDtypeStruct((rows, TILE), f32),
            jax.ShapeDtypeStruct((rows, M2 - TILE), f32),
        ),
        in_specs=[smem, vmem, vmem, vmem, vmem] + [anywhere] * (2 + len(edges)),
        out_specs=(anywhere, anywhere, anywhere),
        scratch_shapes=[
            pltpu.VMEM((2, devices) + edge.shape, f32),
            pltpu.VMEM((sent, width), f32),
            pltpu.VMEM(far.shape, f32),
            pltpu.VMEM((rows, separator), f32),
            pltpu.VMEM((rows, TILE), f32),
            pltpu.VMEM((2, devices, sent, separator), bf16),
            pltpu.VMEM((2, devices, sent, separator), bf16),
            pltpu.VMEM((M2, TILE), f32),
            pltpu.VMEM((M2, 3 * TILE), bf16),
            pltpu.VMEM((M2, 3 * TILE), bf16),
            pltpu.VMEM((rows + TILE, M2), f32),
            pltpu.VMEM((1, TILE, TILE), f32),
            pltpu.SemaphoreType.DMA((len(edges),)),
            pltpu.SemaphoreType.DMA((2,)),
            pltpu.SemaphoreType.DMA((2 + M2 // 512,)),
        ],
        compiler_params=params,
        cost_estimate=pl.CostEstimate(flops=15 * 10**9, bytes_accessed=2**25, transcendentals=0),
        name="parent",
    )(table, heads, weights[None], slab, inverse, matrix, far, *edges)


def on_device(leaf_fronts, screen_weights, parent_tile_index):
    results = [
        one_front(leaf_fronts[0, g], screen_weights[0, g], parent_tile_index[:, g])
        for g in range(leaf_fronts.shape[1])
    ]
    return tuple(jnp.stack(parts)[None] for parts in zip(*results))


def solution(mesh):
    in_specs = (P("leaf", None, "front", None), P("leaf", None, "front"), P())
    out_specs = (
        P("leaf", None, "front", None),
        P("leaf", None, "front", None),
        P("leaf", None, "front", None),
    )
    return jax.shard_map(
        on_device, mesh=mesh, in_specs=in_specs, out_specs=out_specs, check_vma=False
    )
```

profile of v0, /device:TPU:0, one launch (start us, length us, event | category | flops | bytes accessed | tf_op | source)
XLA Modules:
  0.0 126.7 jit_solution(17223943304105811897)
XLA Ops:
  0.6 0.0 copy-start.2
  0.6 1.3 %slice_bitcast_fusion.1 = f32[128,2048]{1,0:T(8,128)S(1)} fusion(f32[1,1,512,2048]{3,2,1,0:T(8,128)} %param.3), kind=kLoop, calls=%fused_computation.3 | loop fusion | bytes 2097152 | tf_op jit(solution)/shard_map/slice | solution.py:371
  2.1 3.0 %collective-permute-start.1 = (f32[136,512]{1,0:T(8,128)S(1)}, f32[136,512]{1,0:T(8,128)S(1)}, u32[]{:S(2)}, u32[]{:S(2)}) collective-permute-start(f32[136,512]{1,0:T(8,128)S(1)} %get-tuple-element.37.refs_3_), channel_id=1, source_target_pairs={{0,4},{4,0},{8,12},{12,8},{16,20},{20,16},{24,28},{28,24},{1,5},{5... | collective-permute-start | bytes 835592 | tf_op jit(solution)/shard_map/ppermute | solution.py:30
  5.1 1.5 %collective-permute-start = (f32[136,512]{1,0:T(8,128)S(1)}, f32[136,512]{1,0:T(8,128)S(1)}, u32[]{:S(2)}, u32[]{:S(2)}) collective-permute-start(f32[136,512]{1,0:T(8,128)S(1)} %get-tuple-element.37.refs_3_), channel_id=1, source_target_pairs={{0,2},{1,3},{2,0},{3,1},{4,6},{5,7},{6,4},{7,5},{8,10},{9,11},{10,... | collective-permute-start | bytes 835592 | tf_op jit(solution)/shard_map/ppermute | solution.py:25
  6.6 2.1 %slice_bitcast_fusion = f32[384,2048]{1,0:T(8,128)S(1)} fusion(f32[1,1,512,2048]{3,2,1,0:T(8,128)} %param.3), kind=kLoop, calls=%fused_computation | loop fusion | bytes 6291456 | tf_op jit(solution)/shard_map/slice | solution.py:372
  8.7 3.1 %collective-permute-done.1 = f32[136,512]{1,0:T(8,128)S(1)} collective-permute-done((f32[136,512]{1,0:T(8,128)S(1)}, f32[136,512]{1,0:T(8,128)S(1)}, u32[]{:S(2)}, u32[]{:S(2)}) %collective-permute-start.1) | collective-permute-done | bytes 278560 | tf_op jit(solution)/shard_map/ppermute | solution.py:30
  11.8 1.7 %collective-permute-start.2 = (f32[136,512]{1,0:T(8,128)S(1)}, f32[136,512]{1,0:T(8,128)S(1)}, u32[]{:S(2)}, u32[]{:S(2)}) collective-permute-start(f32[136,512]{1,0:T(8,128)S(1)} %collective-permute-done.1), channel_id=1, source_target_pairs={{0,2},{1,3},{2,0},{3,1},{4,6},{5,7},{6,4},{7,5},{8,10},{9,11},{10,... | collective-permute-start | bytes 835592 | tf_op jit(solution)/shard_map/ppermute | solution.py:25
  13.5 0.7 slice_dynamic-update-slice_fusion.4
  14.2 0.7 slice_dynamic-update-slice_fusion.3
  14.9 0.0 collective-permute-done
  14.9 4.7 %collective-permute-done.2 = f32[136,512]{1,0:T(8,128)S(1)} collective-permute-done((f32[136,512]{1,0:T(8,128)S(1)}, f32[136,512]{1,0:T(8,128)S(1)}, u32[]{:S(2)}, u32[]{:S(2)}) %collective-permute-start.2) | collective-permute-done | bytes 278560 | tf_op jit(solution)/shard_map/ppermute | solution.py:25
  19.6 0.1 pad_maximum_fusion.1.refs_0_
  19.7 0.1 collective-permute-start.3
  19.8 0.9 slice_dynamic-update-slice_fusion.2
  20.7 0.8 slice_dynamic-update-slice_fusion.1
  21.5 0.7 slice_dynamic-update-slice_fusion.refs_7_
  22.2 0.2 fusion.1
  22.4 0.1 pad_maximum_fusion
  22.6 1.5 %collective-permute-start.4 = (f32[384,640]{1,0:T(8,128)}, f32[384,640]{1,0:T(8,128)}, u32[]{:S(2)}, u32[]{:S(2)}) collective-permute-start(f32[384,640]{1,0:T(8,128)} %slice_dynamic-update-slice_fusion.refs_7_), channel_id=1, source_target_pairs={{0,4},{4,0},{8,12},{12,8},{16,20},{20,16},{24,28},{28,24},{1,5},{5... | collective-permute-start | bytes 2949128 | tf_op jit(solution)/shard_map/ppermute | solution.py:30
  24.1 0.6 collective-permute-start.5
  24.7 1.4 %collective-permute-start.6 = (f32[384,640]{1,0:T(8,128)}, f32[384,640]{1,0:T(8,128)}, u32[]{:S(2)}, u32[]{:S(2)}) collective-permute-start(f32[384,640]{1,0:T(8,128)} %slice_dynamic-update-slice_fusion.refs_7_), channel_id=1, source_target_pairs={{0,2},{1,3},{2,0},{3,1},{4,6},{5,7},{6,4},{7,5},{8,10},{9,11},{10,... | collective-permute-start | bytes 2949128 | tf_op jit(solution)/shard_map/ppermute | solution.py:25
  26.1 0.0 collective-permute-done.3.refs_1_
  26.1 23.3 %corner_first.1 = (f32[2,512,512]{2,1,0:T(8,128)}, f32[2,512,512]{2,1,0:T(8,128)}, f32[2,8,512]{2,1,0:T(8,128)}) custom-call(f32[4,136,512]{2,1,0:T(8,128)} %copy-done, f32[4,136,512]{2,1,0:T(8,128)} %collective-permute-done.3.refs_1_), custom_call_target="tpu_custom_call" | custom-call | flops 12000000000 | bytes 8388608 | tf_op jit(solution)/shard_map/corner_first/pallas_call | solution.py:394
  49.3 0.6 collective-permute-start.9
  50.0 0.0 collective-permute-start.10
  50.0 0.5 collective-permute-start.7
  50.5 0.0 collective-permute-start.8
  50.5 22.2 %collective-permute-done.9.refs_12_ = f32[384,640]{1,0:T(8,128)S(1)} collective-permute-done((f32[384,640]{1,0:T(8,128)}, f32[384,640]{1,0:T(8,128)S(1)}, u32[]{:S(2)}, u32[]{:S(2)}) %collective-permute-start.9) | collective-permute-done | bytes 983072 | tf_op jit(solution)/shard_map/ppermute | solution.py:25
  72.7 23.8 %corner_second.1.refs_4_ = f32[2,512,512]{2,1,0:T(8,128)} custom-call(f32[2,512,512]{2,1,0:T(8,128)} %get-tuple-element.19.refs_0_, f32[2,512,512]{2,1,0:T(8,128)} %get-tuple-element.20.refs_1_), custom_call_target="tpu_custom_call" | custom-call | flops 12000000000 | bytes 8388608 | tf_op jit(solution)/shard_map/corner_second/pallas_call | solution.py:407
  96.5 0.0 collective-permute-done.7.refs_9_
  96.5 0.9 copy-done.4
  97.5 29.0 %parent.1 = (f32[512,512]{1,0:T(8,128)}, f32[512,128]{1,0:T(8,128)}, f32[512,3968]{1,0:T(8,128)}) custom-call(s32[8,12]{1,0:T(8,128)} %bitcast.21, f32[2,8,512]{2,1,0:T(8,128)} %get-tuple-element.16.refs_1_, f32[1,512]{1,0:T(1,128)} %bitcast.19, f32[136,512]{1,0:T(8,128)} %copy-done.1, f32[2,512,512]{2,1,0:T(8,128)} %corner_second.1.refs_4_, ...), custom_call_target="tpu_custom_call" | custom-call | flops 15000000512 | bytes 33554432 | tf_op jit(solution)/shard_map/parent/pallas_call | solution.py:420
  (18 shorter events, 0.1 us)
Async XLA Ops:
  0.6 1.4 %copy-start.2 = (f32[1,1,512]{2,1,0:T(1,128)S(1)}, f32[1,1,512]{2,1,0:T(1,128)}, u32[]{:S(2)}) copy-start(f32[1,1,512]{2,1,0:T(1,128)} %param.4) | copy-start | bytes 6148
  2.1 6.6 %copy-start.1 = (f32[136,512]{1,0:T(8,128)}, f32[136,512]{1,0:T(8,128)S(1)}, u32[]{:S(2)}) copy-start(f32[136,512]{1,0:T(8,128)S(1)} %get-tuple-element.37.refs_3_) | copy-start | bytes 835588
  2.1 9.7 %collective-permute-start.1 = (f32[136,512]{1,0:T(8,128)S(1)}, f32[136,512]{1,0:T(8,128)S(1)}, u32[]{:S(2)}, u32[]{:S(2)}) collective-permute-start(f32[136,512]{1,0:T(8,128)S(1)} %get-tuple-element.37.refs_3_), channel_id=1, source_target_pairs={{0,4},{4,0},{8,12},{12,8},{16,20},{20,16},{24,28},{28,24},{1,5},{5... | collective-permute-start | bytes 835592 | tf_op jit(solution)/shard_map/ppermute | solution.py:30
  5.1 9.8 %collective-permute-start = (f32[136,512]{1,0:T(8,128)S(1)}, f32[136,512]{1,0:T(8,128)S(1)}, u32[]{:S(2)}, u32[]{:S(2)}) collective-permute-start(f32[136,512]{1,0:T(8,128)S(1)} %get-tuple-element.37.refs_3_), channel_id=1, source_target_pairs={{0,2},{1,3},{2,0},{3,1},{4,6},{5,7},{6,4},{7,5},{8,10},{9,11},{10,... | collective-permute-start | bytes 835592 | tf_op jit(solution)/shard_map/ppermute | solution.py:25
  11.8 7.8 %collective-permute-start.2 = (f32[136,512]{1,0:T(8,128)S(1)}, f32[136,512]{1,0:T(8,128)S(1)}, u32[]{:S(2)}, u32[]{:S(2)}) collective-permute-start(f32[136,512]{1,0:T(8,128)S(1)} %collective-permute-done.1), channel_id=1, source_target_pairs={{0,2},{1,3},{2,0},{3,1},{4,6},{5,7},{6,4},{7,5},{8,10},{9,11},{10,... | collective-permute-start | bytes 835592 | tf_op jit(solution)/shard_map/ppermute | solution.py:25
  19.7 2.7 %copy-start = (f32[4,136,512]{2,1,0:T(8,128)}, f32[4,136,512]{2,1,0:T(8,128)S(1)}, u32[]{:S(2)}) copy-start(f32[4,136,512]{2,1,0:T(8,128)S(1)} %pad_maximum_fusion.1.refs_0_) | copy-start | bytes 3342340
  19.7 6.4 %collective-permute-start.3 = (f32[4,136,512]{2,1,0:T(8,128)S(1)}, f32[4,136,512]{2,1,0:T(8,128)}, u32[]{:S(2)}, u32[]{:S(2)}) collective-permute-start(f32[4,136,512]{2,1,0:T(8,128)S(1)} %pad_maximum_fusion.1.refs_0_), channel_id=1, source_target_pairs={{0,1},{1,0},{2,3},{3,2},{4,5},{5,4},{6,7},{7,6},{8,9},{9,8},{10,11... | collective-permute-start | bytes 3342344 | tf_op jit(solution)/shard_map/ppermute | solution.py:25
  22.6 26.7 %collective-permute-start.4 = (f32[384,640]{1,0:T(8,128)}, f32[384,640]{1,0:T(8,128)}, u32[]{:S(2)}, u32[]{:S(2)}) collective-permute-start(f32[384,640]{1,0:T(8,128)} %slice_dynamic-update-slice_fusion.refs_7_), channel_id=1, source_target_pairs={{0,4},{4,0},{8,12},{12,8},{16,20},{20,16},{24,28},{28,24},{1,5},{5... | collective-permute-start | bytes 2949128 | tf_op jit(solution)/shard_map/ppermute | solution.py:30
  24.1 72.4 %collective-permute-start.5 = (f32[384,1408]{1,0:T(8,128)S(1)}, f32[384,1408]{1,0:T(8,128)}, u32[]{:S(2)}, u32[]{:S(2)}) collective-permute-start(f32[384,1408]{1,0:T(8,128)S(1)} %pad_maximum_fusion), channel_id=1, source_target_pairs={{0,4},{4,0},{8,12},{12,8},{16,20},{20,16},{24,28},{28,24},{1,5},{5... | collective-permute-start | bytes 6488072 | tf_op jit(solution)/shard_map/ppermute | solution.py:30
  24.7 25.8 %collective-permute-start.6 = (f32[384,640]{1,0:T(8,128)}, f32[384,640]{1,0:T(8,128)}, u32[]{:S(2)}, u32[]{:S(2)}) collective-permute-start(f32[384,640]{1,0:T(8,128)} %slice_dynamic-update-slice_fusion.refs_7_), channel_id=1, source_target_pairs={{0,2},{1,3},{2,0},{3,1},{4,6},{5,7},{6,4},{7,5},{8,10},{9,11},{10,... | collective-permute-start | bytes 2949128 | tf_op jit(solution)/shard_map/ppermute | solution.py:25
  49.3 23.4 %collective-permute-start.9 = (f32[384,640]{1,0:T(8,128)}, f32[384,640]{1,0:T(8,128)S(1)}, u32[]{:S(2)}, u32[]{:S(2)}) collective-permute-start(f32[384,640]{1,0:T(8,128)} %collective-permute-done.4.refs_11_), channel_id=1, source_target_pairs={{0,2},{1,3},{2,0},{3,1},{4,6},{5,7},{6,4},{7,5},{8,10},{9,11},{10,... | collective-permute-start | bytes 2949128 | tf_op jit(solution)/shard_map/ppermute | solution.py:25
  50.0 46.5 %collective-permute-start.10 = (f32[384,640]{1,0:T(8,128)}, f32[384,640]{1,0:T(8,128)S(1)}, u32[]{:S(2)}, u32[]{:S(2)}) collective-permute-start(f32[384,640]{1,0:T(8,128)} %collective-permute-done.4.refs_11_), channel_id=1, source_target_pairs={{0,1},{1,0},{2,3},{3,2},{4,5},{5,4},{6,7},{7,6},{8,9},{9,8},{10,11... | collective-permute-start | bytes 2949128 | tf_op jit(solution)/shard_map/ppermute | solution.py:25
  50.0 46.5 %collective-permute-start.7 = (f32[384,640]{1,0:T(8,128)}, f32[384,640]{1,0:T(8,128)}, u32[]{:S(2)}, u32[]{:S(2)}) collective-permute-start(f32[384,640]{1,0:T(8,128)} %slice_dynamic-update-slice_fusion.refs_7_), channel_id=1, source_target_pairs={{0,1},{1,0},{2,3},{3,2},{4,5},{5,4},{6,7},{7,6},{8,9},{9,8},{10,11... | collective-permute-start | bytes 2949128 | tf_op jit(solution)/shard_map/ppermute | solution.py:25
  50.5 46.0 %collective-permute-start.8 = (f32[384,640]{1,0:T(8,128)}, f32[384,640]{1,0:T(8,128)}, u32[]{:S(2)}, u32[]{:S(2)}) collective-permute-start(f32[384,640]{1,0:T(8,128)} %collective-permute-done.6.refs_8_), channel_id=1, source_target_pairs={{0,1},{1,0},{2,3},{3,2},{4,5},{5,4},{6,7},{7,6},{8,9},{9,8},{10,11... | collective-permute-start | bytes 2949128 | tf_op jit(solution)/shard_map/ppermute | solution.py:25
  72.7 23.8 %copy-start.3 = (f32[384,640]{1,0:T(8,128)}, f32[384,640]{1,0:T(8,128)S(1)}, u32[]{:S(2)}) copy-start(f32[384,640]{1,0:T(8,128)S(1)} %collective-permute-done.9.refs_12_) | copy-start | bytes 2949124
  72.7 23.8 %collective-permute-start.11 = (f32[384,640]{1,0:T(8,128)S(1)}, f32[384,640]{1,0:T(8,128)}, u32[]{:S(2)}, u32[]{:S(2)}) collective-permute-start(f32[384,640]{1,0:T(8,128)S(1)} %collective-permute-done.9.refs_12_), channel_id=1, source_target_pairs={{0,1},{1,0},{2,3},{3,2},{4,5},{5,4},{6,7},{7,6},{8,9},{9,8},{10,11... | collective-permute-start | bytes 2949128 | tf_op jit(solution)/shard_map/ppermute | solution.py:25
  96.5 1.0 copy-start.4
where the time goes:
time: 127 us
  Pallas kernels  76.1 us (60%)
  waiting for transfers between devices  30 us (24%)
  starting transfers between devices  10.9 us (9%)
  local copies, waits for them, and re-layouts  8.47 us (7%)
    pallas_call x1, Pallas kernels, one_front(): pl.pallas_call(functools.partial(parent_kernel, count=count, skip=skip, w...  29 us
    ppermute x9, waiting for transfers between devices, from_front(): return lax.ppermute(value, 'front', pairs)  26.9 us
    pallas_call x1, Pallas kernels, one_front(): pl.pallas_call(functools.partial(half_kernel, first=middle, last=separato...  23.8 us
    pallas_call x1, Pallas kernels, one_front(): pl.pallas_call(functools.partial(half_kernel, first=0, last=middle), out_...  23.3 us
    ppermute x9, starting transfers between devices, from_front(): return lax.ppermute(value, 'front', pairs)  5.82 us
    ppermute x3, starting transfers between devices, from_sibling(): return lax.ppermute(value, 'leaf', pairs)  5.12 us
    unnamed x14, local copies, waits for them, and re-layouts  4.08 us
    ppermute x3, waiting for transfers between devices, from_sibling(): return lax.ppermute(value, 'leaf', pairs)  3.06 us
  transfers between devices with their start and end apart: 12, of which 3 were waited for; matrix products, arithmetic and copies ran while one was open for 5% of the time, Pallas kernels for 37%

commit v1 on v0

--- a/solution.py
+++ b/solution.py
@@ -12,12 +12,14 @@
 M2 = 4096
 GROUP_TILES = 4
 SLAB = 8
+GROUP = 32
 EXACT = lax.Precision.HIGHEST
 VMEM_BYTES = 60 * 2**20
 
 TILE = PANEL_WIDTH
 LAST = ((1,), (1,))
 PLAIN = ((1,), (0,))
+FIRST = ((0,), (0,))
 
 
 def from_front(value, distance):
@@ -79,12 +81,9 @@
     return terms[0]
 
 
-def factor_slab(block, first, inside, lanes):
-    rows = [jnp.broadcast_to(block[i : i + 1, :], block.shape) for i in range(SLAB)]
+def factor_slab(rows, first, inside, lanes):
     entry = {(i, j): lane(rows[i], first + j) for i in range(SLAB) for j in range(i + 1)}
-    rows = [
-        jnp.where(inside, jnp.where(lanes == first + i, 1.0, 0.0), row) for i, row in enumerate(rows)
-    ]
+    rows = [jnp.where(inside, jnp.where(lanes == first + i, 1.0, 0.0), row) for i, row in enumerate(rows)]
     done = []
     for p in range(0, SLAB, 2):
         r = p + 1
@@ -106,21 +105,36 @@
 
 
 def factor_steps(a, fronts):
-    sublanes = lax.broadcasted_iota(jnp.int32, (SLAB, TILE), 0)
-    lanes = lax.broadcasted_iota(jnp.int32, (SLAB, TILE), 1)
-    for start in range(0, TILE, SLAB):
-        inside = (lanes >= start) & (lanes < start + SLAB)
-        for q in range(fronts):
-            rows = factor_slab(a[q, start : start + SLAB, :], start, inside, lanes)
-            for low in range(start + SLAB, TILE, SLAB):
-                chosen = sublanes + low
-                terms = [jnp.take_along_axis(row, chosen, axis=1) * row for row in rows]
-                block = a[q, low : low + SLAB, :]
-                a[q, low : low + SLAB, :] = jnp.where(inside, 0.0, block) - sum_tree(terms)
-            block = rows[0]
-            for i in range(1, SLAB):
-                block = jnp.where(sublanes == i, rows[i], block)
-            a[q, start : start + SLAB, :] = block
+    lanes = lax.broadcasted_iota(jnp.int32, (fronts, TILE), 1)
+    columns = lax.broadcasted_iota(jnp.int32, (TILE, TILE), 1)
+    settled = (lax.broadcasted_iota(jnp.int32, (GROUP, TILE), 0) & -SLAB) + SLAB
+
+    def at(i):
+        return pl.ds(fronts * i, fronts)
+
+    for start in range(0, TILE, GROUP):
+        stop = start + GROUP
+        rows = [a[at(i), :] for i in range(start, stop)]
+        for s in range(0, GROUP, SLAB):
+            first = start + s
+            inside = (lanes >= first) & (lanes < first + SLAB)
+            head = factor_slab(rows[s : s + SLAB], first, inside, lanes)
+            for i in range(SLAB):
+                a[at(first + i), :] = head[i]
+            for i in range(s + SLAB, GROUP):
+                terms = [lane(row, start + i) * row for row in head]
+                rows[i] = jnp.where(inside, 0.0, rows[i]) - sum_tree(terms)
+            if s + SLAB < GROUP:
+                yield
+        if stop < TILE:
+            for q in range(fronts):
+                upper = a[pl.ds(fronts * start + q, GROUP, stride=fronts), :]
+                rest = pl.ds(fronts * stop + q, TILE - stop, stride=fronts)
+                inverse = jnp.where((columns[:GROUP] >= start + settled) & (columns[:GROUP] < stop), 0.0, upper)
+                product = exact_dot(upper, inverse, FIRST)[stop:]
+                group = columns[stop:]
+                kept = jnp.where((group >= start) & (group < stop), 0.0, a[rest, :])
+                a[rest, :] = kept - product
         yield
 
 
@@ -131,22 +145,22 @@
 
 def corner_kernel(*refs, order, first, last, count, devices):
     tiles = order // TILE
+    pieces = 2 * devices
     if first == 0:
-        near, other, work, out, heads, a = refs
+        slabs, (work, out, heads, a) = refs[:pieces], refs[pieces:]
     else:
         old_work, old_out, out, work, a = refs
     fronts = out.shape[0]
     if first == 0:
         front = place()[1]
-        pieces = devices // 2
 
         def copy(owner, q, take):
             slot = slot_of(front ^ owner, devices)
-            for held, low in ((near, 0), (other, pieces)):
-
-                @pl.when((slot >= low) & (slot < low + pieces))
+            for s in range(devices):
+
+                @pl.when(slot == s)
                 def _():
-                    take(held.at[q * pieces + slot - low])
+                    take(slabs[q * devices + s])
 
         for q in range(fronts):
             for e in range(tiles):
@@ -167,12 +181,12 @@
     def step(k, carry):
         block = pl.ds(pl.multiple_of(k * TILE, TILE), TILE)
         for q in range(fronts):
-            a[q] = work[q, block, block]
+            a[pl.ds(q, TILE, stride=fronts), :] = work[q, block, block]
         for _ in factor_steps(a, fronts):
             pass
         kept = lax.broadcasted_iota(jnp.int32, (TILE, TILE), 0) >= lax.broadcasted_iota(jnp.int32, (TILE, TILE), 1)
         for q in range(fronts):
-            out[q, block, block] = jnp.where(kept, a[q], 0.0)
+            out[q, block, block] = jnp.where(kept, a[pl.ds(q, TILE, stride=fronts), :], 0.0)
         for fixed in range(first, last):
 
             @pl.when(k == fixed)
@@ -310,7 +324,7 @@
                 total[at(target), at(goal)] += source - product[line, c * TILE : (c + 1) * TILE]
 
     work = [functools.partial(contribution, i, s) for i in range(2) for s in range(devices)]
-    a[0] = column[:TILE, :]
+    a[...] = column[:TILE, :]
     steps = TILE // SLAB
     for k, _ in enumerate(factor_steps(a, 1)):
         while work and len(work) * steps >= (steps - k) * (2 * devices):
@@ -318,7 +332,7 @@
     for task in work:
         task()
 
-    turned = halves(jnp.where(row_ids >= col_ids, a[0], 0.0))
+    turned = halves(jnp.where(row_ids >= col_ids, a[...], 0.0))
     for start in range(0, M2, 1024):
         block = slice(start, start + 1024)
         panel = split_dot(halves(column[block, :]), turned)
@@ -346,6 +360,43 @@
         send.wait()
 
 
+def slab_kernel(matrix, weights, slab, done, *, chosen):
+    copies = [
+        pltpu.make_async_copy(
+            matrix.at[:TILE, t * TILE : (t + 1) * TILE], slab.at[:TILE, k * TILE : (k + 1) * TILE], done.at[k]
+        )
+        for k, t in enumerate(chosen)
+    ]
+    for copy in copies:
+        copy.start()
+    slab[TILE:, :] = jnp.zeros_like(slab[TILE:, :])
+    slab[TILE : TILE + 1, : weights.shape[1]] = weights[...]
+    for copy in copies:
+        copy.wait()
+
+
+def body_kernel(matrix, edge, far, done, *, skip, chosen, rest):
+    copies = []
+    for target, tiles in ((edge, chosen), (far, rest)):
+        filled = 0
+        while filled < len(tiles):
+            stop = filled + 1
+            while stop < len(tiles) and tiles[stop] == tiles[stop - 1] + 1:
+                stop += 1
+            copies.append(
+                pltpu.make_async_copy(
+                    matrix.at[skip * TILE :, tiles[filled] * TILE : (tiles[stop - 1] + 1) * TILE],
+                    target.at[:, filled * TILE : stop * TILE],
+                    done.at[len(copies)],
+                )
+            )
+            filled = stop
+    for copy in copies:
+        copy.start()
+    for copy in copies:
+        copy.wait()
+
+
 def one_front(matrix, weights, table):
     rows, width = matrix.shape
     devices = lax.axis_size("front")
@@ -357,50 +408,67 @@
     while 2 ** (len(distances) + 1) < devices:
         distances.insert(0, 2 ** (len(distances) + 1))
 
-    def columns(block, chosen):
-        return jnp.concatenate([block[:, t * TILE : (t + 1) * TILE] for t in chosen], axis=1)
-
     def spread(pieces):
         for distance in distances:
             pieces = pieces + [from_front(piece, distance) for piece in pieces]
         return pieces
 
-    corner = list(range(0, tiles, GROUP_TILES))
-    rest = [t for t in range(tiles) if t % GROUP_TILES and t != 1]
-    weight_rows = jnp.pad(weights[None], ((0, SLAB - 1), (0, separator - rows)))
-    slab = jnp.concatenate([columns(matrix[:TILE], corner), weight_rows], axis=0)
-    body = matrix[skip * TILE :]
-    far_slab = from_sibling(slab)
-    slabs = spread([slab])
-    edge = columns(body, corner + [1])
-    far_body = columns(body, rest)
-    far_slabs = spread([far_slab])
-    held = jnp.stack(slabs + far_slabs)
-    other = from_front(held, 1)
-    far_edge = from_sibling(after(edge, far_slab))
-    far = from_sibling(after(far_body, far_slab))
-    near_edges = spread([after(edge, *far_slabs)])
-
     vmem = pl.BlockSpec(memory_space=pltpu.VMEM)
     smem = pl.BlockSpec(memory_space=pltpu.SMEM)
     anywhere = pl.BlockSpec(memory_space=pl.ANY)
     f32, bf16 = jnp.float32, jnp.bfloat16
+    params = pltpu.CompilerParams(vmem_limit_bytes=VMEM_BYTES)
+    small = pltpu.CompilerParams(vmem_limit_bytes=VMEM_BYTES // 3)
+
+    corner = list(range(0, tiles, GROUP_TILES))
+    rest = [t for t in range(tiles) if t % GROUP_TILES and t != 1]
+    slab = pl.pallas_call(
+        functools.partial(slab_kernel, chosen=corner),
+        out_shape=jax.ShapeDtypeStruct((TILE + SLAB, separator), f32),
+        in_specs=[anywhere, vmem],
+        out_specs=vmem,
+        scratch_shapes=[pltpu.SemaphoreType.DMA((len(corner),))],
+        compiler_params=params,
+        cost_estimate=pl.CostEstimate(flops=0, bytes_accessed=2**19, transcendentals=0),
+        name="slab",
+    )(matrix, weights[None])
+    far_slab = from_sibling(slab)
+    slabs = spread([slab])
+    edge, far_body = pl.pallas_call(
+        functools.partial(body_kernel, skip=skip, chosen=corner + [1], rest=rest),
+        out_shape=(
+            jax.ShapeDtypeStruct((sent, (len(corner) + 1) * TILE), f32),
+            jax.ShapeDtypeStruct((sent, len(rest) * TILE), f32),
+        ),
+        in_specs=[anywhere],
+        out_specs=(anywhere, anywhere),
+        scratch_shapes=[pltpu.SemaphoreType.DMA((2 * tiles,))],
+        compiler_params=params,
+        cost_estimate=pl.CostEstimate(flops=0, bytes_accessed=2**23, transcendentals=0),
+        name="body",
+    )(after(matrix, slab))
+    far_slabs = spread([after(far_slab, edge)])
+    other_slabs = [from_front(piece, 1) for piece in slabs]
+    other_far_slabs = [from_front(piece, 1) for piece in far_slabs]
+    far_edge = from_sibling(after(edge, far_slab))
+    far = from_sibling(after(far_body, far_slab))
+    near_edges = spread([after(edge, *far_slabs)])
+
     state = jax.ShapeDtypeStruct((2, separator, separator), f32)
-    scratch = pltpu.VMEM((2, TILE, TILE), f32)
-    params = pltpu.CompilerParams(vmem_limit_bytes=VMEM_BYTES)
+    scratch = pltpu.VMEM((2 * TILE, TILE), f32)
     cost = pl.CostEstimate(flops=12 * 10**9, bytes_accessed=2**23, transcendentals=0)
     middle = separator // TILE // 2
     half_kernel = functools.partial(corner_kernel, order=separator, count=count, devices=devices)
     state_one, state_two, heads = pl.pallas_call(
         functools.partial(half_kernel, first=0, last=middle),
         out_shape=(state, state, jax.ShapeDtypeStruct((2, SLAB, separator), f32)),
-        in_specs=[vmem, vmem],
+        in_specs=[vmem] * (2 * devices),
         out_specs=(vmem, vmem, vmem),
         scratch_shapes=[scratch],
-        compiler_params=params,
+        compiler_params=small,
         cost_estimate=cost,
         name="corner_first",
-    )(held, other)
+    )(*slabs, *other_slabs, *far_slabs, *other_far_slabs)
 
     other_edges = [from_front(after(piece, heads), 1) for piece in near_edges]
     far_edges = spread([after(far_edge, heads)])
@@ -410,11 +478,11 @@
         in_specs=[vmem, vmem],
         out_specs=vmem,
         scratch_shapes=[pltpu.VMEM((2, separator, separator), f32), scratch],
-        compiler_params=params,
+        compiler_params=small,
         cost_estimate=cost,
         name="corner_second",
     )(after(state_one, far_edge), state_two)
-    other_far_edges = [from_front(piece, 1) for piece in far_edges]
+    other_far_edges = [from_front(after(piece, inverse), 1) for piece in far_edges]
 
     edges = near_edges + other_edges + far_edges + other_far_edges
     return pl.pallas_call(
@@ -438,12 +506,12 @@
             pltpu.VMEM((M2, 3 * TILE), bf16),
             pltpu.VMEM((M2, 3 * TILE), bf16),
             pltpu.VMEM((rows + TILE, M2), f32),
-            pltpu.VMEM((1, TILE, TILE), f32),
+            pltpu.VMEM((TILE, TILE), f32),
             pltpu.SemaphoreType.DMA((len(edges),)),
             pltpu.SemaphoreType.DMA((2,)),
             pltpu.SemaphoreType.DMA((2 + M2 // 512,)),
         ],
-        compiler_params=params,
+        compiler_params=pltpu.CompilerParams(vmem_limit_bytes=VMEM_BYTES * 3 // 4),
         cost_estimate=pl.CostEstimate(flops=15 * 10**9, bytes_accessed=2**25, transcendentals=0),
         name="parent",
     )(table, heads, weights[None], slab, inverse, matrix, far, *edges)

time: 127 us -> 216 us (1.70)
  Pallas kernels: 76.1 us -> 160 us
  waiting for transfers between devices: 30 us -> 42.5 us
  local copies, waits for them, and re-layouts: 8.47 us -> 2.64 us
    pallas_call x0 -> x2, Pallas kernels: none -> 99 us  [the longest x1 96.7 us: one_front(): pl.pallas_call(functools.partial(body_kernel, skip=skip, chosen=corner +...]
    ppermute x3, waiting for transfers between devices: 3.06 us -> 30.2 us  [from_sibling(): return lax.ppermute(value, 'leaf', pairs)]
    ppermute x9 -> x12, waiting for transfers between devices: 26.9 us -> 12.3 us  [from_front(): return lax.ppermute(value, 'front', pairs)]
    pallas_call x1, Pallas kernels: 23.8 us -> 15 us  [one_front(): pl.pallas_call(functools.partial(half_kernel, first=middle, last=separato...]
    pallas_call x1, Pallas kernels: 23.3 us -> 14.9 us  [one_front(): pl.pallas_call(functools.partial(half_kernel, first=0, last=middle), out_...]
    slice x5 -> x0, local copies, waits for them, and re-layouts: 3.64 us -> none  [the longest x1 2.09 us: one_front(): body = matrix[skip * TILE:]]
    pallas_call x1, Pallas kernels: 29 us -> 31.3 us  [one_front(): pl.pallas_call(functools.partial(parent_kernel, count=count, skip=skip, w...]
    ppermute x9 -> x12, starting transfers between devices: 5.82 us -> 4.33 us  [from_front(): return lax.ppermute(value, 'front', pairs)]
  transfers between devices with their start and end apart: 12 -> 15, of which waited for: 3 -> 4; matrix products, arithmetic and copies ran while one was open for 5% -> 0% of each run, Pallas kernels for 37% -> 59%
where the time goes in v1:
time: 216 us
  Pallas kernels  160 us (74%)
  waiting for transfers between devices  42.5 us (20%)
  starting transfers between devices  9.38 us (4%)
  local copies, waits for them, and re-layouts  2.64 us (1%)
    pallas_call x1, Pallas kernels, one_front(): pl.pallas_call(functools.partial(body_kernel, skip=skip, chosen=corner +...  96.7 us
    pallas_call x1, Pallas kernels, one_front(): pl.pallas_call(functools.partial(parent_kernel, count=count, skip=skip, w...  31.3 us
    ppermute x3, waiting for transfers between devices, from_sibling(): return lax.ppermute(value, 'leaf', pairs)  30.2 us
    pallas_call x1, Pallas kernels, one_front(): pl.pallas_call(functools.partial(half_kernel, first=middle, last=separato...  15 us
    pallas_call x1, Pallas kernels, one_front(): pl.pallas_call(functools.partial(half_kernel, first=0, last=middle), out_...  14.9 us
    ppermute x12, waiting for transfers between devices, from_front(): return lax.ppermute(value, 'front', pairs)  12.3 us
    ppermute x3, starting transfers between devices, from_sibling(): return lax.ppermute(value, 'leaf', pairs)  5.06 us
    ppermute x12, starting transfers between devices, from_front(): return lax.ppermute(value, 'front', pairs)  4.33 us
  transfers between devices with their start and end apart: 15, of which 4 were waited for; matrix products, arithmetic and copies ran while one was open for 0% of the time, Pallas kernels for 59%

profile of v1, /device:TPU:0, one launch (start us, length us, event | category | flops | bytes accessed | tf_op | source)
XLA Modules:
  0.0 215.7 jit_solution(13146379957493366372)
XLA Ops:
  0.6 2.4 %slab.1.refs_0_.refs_3_ = f32[136,512]{1,0:T(8,128)} custom-call(f32[512,2048]{1,0:T(8,128)} %bitcast.9, f32[1,512]{1,0:T(1,128)} %bitcast.6), custom_call_target="tpu_custom_call" | custom-call | bytes 524288 | tf_op jit(solution)/shard_map/slab/pallas_call | solution.py:425
  3.0 3.0 %collective-permute-start.3 = (f32[136,512]{1,0:T(8,128)}, f32[136,512]{1,0:T(8,128)S(1)}, u32[]{:S(2)}, u32[]{:S(2)}) collective-permute-start(f32[136,512]{1,0:T(8,128)} %slab.1.refs_0_.refs_3_), channel_id=1, source_target_pairs={{0,4},{4,0},{8,12},{12,8},{16,20},{20,16},{24,28},{28,24},{1,5},{5... | collective-permute-start | bytes 835592 | tf_op jit(solution)/shard_map/ppermute | solution.py:32
  6.0 1.5 collective-permute-start
  7.5 96.7 %body.1 = (f32[384,640]{1,0:T(8,128)}, f32[384,1408]{1,0:T(8,128)}) custom-call(f32[512,2048]{1,0:T(8,128)} %bitcast.10), custom_call_target="tpu_custom_call" | custom-call | bytes 8388608 | tf_op jit(solution)/shard_map/body/pallas_call | solution.py:437
  104.2 0.0 collective-permute-done.3.refs_4_
  104.2 0.6 collective-permute-start.4
  104.8 0.0 collective-permute-start.1
  104.8 0.0 collective-permute-done.refs_1_
  104.8 0.5 collective-permute-start.2
  105.4 0.1 collective-permute-start.5
  105.4 6.7 %collective-permute-done.4.refs_5_ = f32[136,512]{1,0:T(8,128)S(1)} collective-permute-done((f32[136,512]{1,0:T(8,128)S(1)}, f32[136,512]{1,0:T(8,128)S(1)}, u32[]{:S(2)}, u32[]{:S(2)}) %collective-permute-start.4) | collective-permute-done | bytes 278560 | tf_op jit(solution)/shard_map/ppermute | solution.py:27
  112.1 0.0 collective-permute-start.6
  112.1 0.5 collective-permute-start.7
  112.7 0.0 collective-permute-done.1.refs_2_
  112.7 1.5 collective-permute-start.8
  114.2 0.0 collective-permute-done.2.refs_3_
  114.2 0.5 collective-permute-start.9
  114.7 0.0 collective-permute-done.5.refs_6_
  114.7 0.0 collective-permute-done.6.refs_7_
  114.7 14.9 %corner_first.1 = (f32[2,512,512]{2,1,0:T(8,128)S(1)}, f32[2,512,512]{2,1,0:T(8,128)S(1)}, f32[2,8,512]{2,1,0:T(8,128)S(1)}) custom-call(f32[136,512]{1,0:T(8,128)S(1)} %copy-done, f32[136,512]{1,0:T(8,128)S(1)} %collective-permute-done.refs_1_, f32[136,512]{1,0:T(8,128)S(1)} %collective-permute-done.1.refs_2_, ...), custom_call_target="tpu_custom_call" | custom-call | flops 12000000000 | bytes 8388608 | tf_op jit(solution)/shard_map/corner_first/pallas_call | solution.py:462
  129.6 0.1 collective-permute-start.10
  129.7 7.2 %collective-permute-done.7.refs_11_ = f32[384,640]{1,0:T(8,128)S(1)} collective-permute-done((f32[384,640]{1,0:T(8,128)}, f32[384,640]{1,0:T(8,128)S(1)}, u32[]{:S(2)}, u32[]{:S(2)}) %collective-permute-start.7) | collective-permute-done | bytes 983072 | tf_op jit(solution)/shard_map/ppermute | solution.py:32
  136.9 0.5 collective-permute-start.12
  137.4 15.0 %corner_second.1.refs_4_ = f32[2,512,512]{2,1,0:T(8,128)S(1)} custom-call(f32[2,512,512]{2,1,0:T(8,128)S(1)} %get-tuple-element.28.refs_0_, f32[2,512,512]{2,1,0:T(8,128)S(1)} %get-tuple-element.29.refs_1_), custom_call_target="tpu_custom_call" | custom-call | flops 12000000000 | bytes 8388608 | tf_op jit(solution)/shard_map/corner_second/pallas_call | solution.py:475
  152.5 1.3 copy-done.4
  153.8 0.5 collective-permute-start.11
  154.3 5.6 %collective-permute-done.12.refs_12_ = f32[384,640]{1,0:T(8,128)S(1)} collective-permute-done((f32[384,640]{1,0:T(8,128)S(1)}, f32[384,640]{1,0:T(8,128)S(1)}, u32[]{:S(2)}, u32[]{:S(2)}) %collective-permute-start.12) | collective-permute-done | bytes 983072 | tf_op jit(solution)/shard_map/ppermute | solution.py:27
  159.9 0.0 collective-permute-done.10.refs_9_
  159.9 0.0 collective-permute-done.13.refs_13_
  159.9 22.9 %collective-permute-done.8.refs_6_ = f32[384,1408]{1,0:T(8,128)S(1)} collective-permute-done((f32[384,1408]{1,0:T(8,128)}, f32[384,1408]{1,0:T(8,128)S(1)}, u32[]{:S(2)}, u32[]{:S(2)}) %collective-permute-start.8) | collective-permute-done | bytes 2162720 | tf_op jit(solution)/shard_map/ppermute | solution.py:32
  182.9 1.3 copy-done.5
  184.2 31.3 %parent.1 = (f32[512,512]{1,0:T(8,128)}, f32[512,128]{1,0:T(8,128)}, f32[512,3968]{1,0:T(8,128)}) custom-call(s32[8,12]{1,0:T(8,128)S(1)} %bitcast.8, f32[2,8,512]{2,1,0:T(8,128)S(1)} %get-tuple-element.25.refs_1_, f32[1,512]{1,0:T(1,128)S(1)} %bitcast.7, f32[136,512]{1,0:T(8,128)S(1)} %copy-done, f32[2,512,512]{2,1,0:T(8,128)} %copy-done.4, ...), custom_call_target="tpu_custom_call" | custom-call | flops 15000000512 | bytes 33554432 | tf_op jit(solution)/shard_map/parent/pallas_call | solution.py:488
  (15 shorter events, 0.0 us)
Async XLA Ops:
  3.0 101.8 %copy-start = (f32[136,512]{1,0:T(8,128)S(1)}, f32[136,512]{1,0:T(8,128)}, u32[]{:S(2)}) copy-start(f32[136,512]{1,0:T(8,128)} %slab.1.refs_0_.refs_3_) | copy-start | bytes 835588
  3.0 101.2 %collective-permute-start.3 = (f32[136,512]{1,0:T(8,128)}, f32[136,512]{1,0:T(8,128)S(1)}, u32[]{:S(2)}, u32[]{:S(2)}) collective-permute-start(f32[136,512]{1,0:T(8,128)} %slab.1.refs_0_.refs_3_), channel_id=1, source_target_pairs={{0,4},{4,0},{8,12},{12,8},{16,20},{20,16},{24,28},{28,24},{1,5},{5... | collective-permute-start | bytes 835592 | tf_op jit(solution)/shard_map/ppermute | solution.py:32
  6.0 98.8 %collective-permute-start = (f32[136,512]{1,0:T(8,128)}, f32[136,512]{1,0:T(8,128)S(1)}, u32[]{:S(2)}, u32[]{:S(2)}) collective-permute-start(f32[136,512]{1,0:T(8,128)} %slab.1.refs_0_.refs_3_), channel_id=1, source_target_pairs={{0,2},{1,3},{2,0},{3,1},{4,6},{5,7},{6,4},{7,5},{8,10},{9,11},{10,... | collective-permute-start | bytes 835592 | tf_op jit(solution)/shard_map/ppermute | solution.py:27
  104.2 7.9 %collective-permute-start.4 = (f32[136,512]{1,0:T(8,128)S(1)}, f32[136,512]{1,0:T(8,128)S(1)}, u32[]{:S(2)}, u32[]{:S(2)}) collective-permute-start(f32[136,512]{1,0:T(8,128)S(1)} %collective-permute-done.3.refs_4_), channel_id=1, source_target_pairs={{0,2},{1,3},{2,0},{3,1},{4,6},{5,7},{6,4},{7,5},{8,10},{9,11},{10,... | collective-permute-start | bytes 835592 | tf_op jit(solution)/shard_map/ppermute | solution.py:27
  104.8 7.8 %collective-permute-start.1 = (f32[136,512]{1,0:T(8,128)S(1)}, f32[136,512]{1,0:T(8,128)S(1)}, u32[]{:S(2)}, u32[]{:S(2)}) collective-permute-start(f32[136,512]{1,0:T(8,128)S(1)} %copy-done), channel_id=1, source_target_pairs={{0,1},{1,0},{2,3},{3,2},{4,5},{5,4},{6,7},{7,6},{8,9},{9,8},{10,11... | collective-permute-start | bytes 835592 | tf_op jit(solution)/shard_map/ppermute | solution.py:27
  104.8 9.3 %collective-permute-start.2 = (f32[136,512]{1,0:T(8,128)S(1)}, f32[136,512]{1,0:T(8,128)S(1)}, u32[]{:S(2)}, u32[]{:S(2)}) collective-permute-start(f32[136,512]{1,0:T(8,128)S(1)} %collective-permute-done.refs_1_), channel_id=1, source_target_pairs={{0,1},{1,0},{2,3},{3,2},{4,5},{5,4},{6,7},{7,6},{8,9},{9,8},{10,11... | collective-permute-start | bytes 835592 | tf_op jit(solution)/shard_map/ppermute | solution.py:27
  105.4 9.4 %collective-permute-start.5 = (f32[136,512]{1,0:T(8,128)S(1)}, f32[136,512]{1,0:T(8,128)S(1)}, u32[]{:S(2)}, u32[]{:S(2)}) collective-permute-start(f32[136,512]{1,0:T(8,128)S(1)} %collective-permute-done.3.refs_4_), channel_id=1, source_target_pairs={{0,1},{1,0},{2,3},{3,2},{4,5},{5,4},{6,7},{7,6},{8,9},{9,8},{10,11... | collective-permute-start | bytes 835592 | tf_op jit(solution)/shard_map/ppermute | solution.py:27
  112.1 2.6 %collective-permute-start.6 = (f32[136,512]{1,0:T(8,128)S(1)}, f32[136,512]{1,0:T(8,128)S(1)}, u32[]{:S(2)}, u32[]{:S(2)}) collective-permute-start(f32[136,512]{1,0:T(8,128)S(1)} %collective-permute-done.4.refs_5_), channel_id=1, source_target_pairs={{0,1},{1,0},{2,3},{3,2},{4,5},{5,4},{6,7},{7,6},{8,9},{9,8},{10,11... | collective-permute-start | bytes 835592 | tf_op jit(solution)/shard_map/ppermute | solution.py:27
  112.1 17.5 %copy-start.2 = (f32[384,640]{1,0:T(8,128)S(1)}, f32[384,640]{1,0:T(8,128)}, u32[]{:S(2)}) copy-start(f32[384,640]{1,0:T(8,128)} %get-tuple-element.33.refs_7_) | copy-start | bytes 2949124
  112.1 24.8 %collective-permute-start.7 = (f32[384,640]{1,0:T(8,128)}, f32[384,640]{1,0:T(8,128)S(1)}, u32[]{:S(2)}, u32[]{:S(2)}) collective-permute-start(f32[384,640]{1,0:T(8,128)} %get-tuple-element.33.refs_7_), channel_id=1, source_target_pairs={{0,4},{4,0},{8,12},{12,8},{16,20},{20,16},{24,28},{28,24},{1,5},{5... | collective-permute-start | bytes 2949128 | tf_op jit(solution)/shard_map/ppermute | solution.py:32
  112.7 70.2 %collective-permute-start.8 = (f32[384,1408]{1,0:T(8,128)}, f32[384,1408]{1,0:T(8,128)S(1)}, u32[]{:S(2)}, u32[]{:S(2)}) collective-permute-start(f32[384,1408]{1,0:T(8,128)} %get-tuple-element.31), channel_id=1, source_target_pairs={{0,4},{4,0},{8,12},{12,8},{16,20},{20,16},{24,28},{28,24},{1,5},{5... | collective-permute-start | bytes 6488072 | tf_op jit(solution)/shard_map/ppermute | solution.py:32
  114.2 39.6 %collective-permute-start.9 = (f32[384,640]{1,0:T(8,128)}, f32[384,640]{1,0:T(8,128)S(1)}, u32[]{:S(2)}, u32[]{:S(2)}) collective-permute-start(f32[384,640]{1,0:T(8,128)} %get-tuple-element.33.refs_7_), channel_id=1, source_target_pairs={{0,2},{1,3},{2,0},{3,1},{4,6},{5,7},{6,4},{7,5},{8,10},{9,11},{10,... | collective-permute-start | bytes 2949128 | tf_op jit(solution)/shard_map/ppermute | solution.py:27
  129.6 30.3 %collective-permute-start.10 = (f32[384,640]{1,0:T(8,128)S(1)}, f32[384,640]{1,0:T(8,128)S(1)}, u32[]{:S(2)}, u32[]{:S(2)}) collective-permute-start(f32[384,640]{1,0:T(8,128)S(1)} %copy-done.2), channel_id=1, source_target_pairs={{0,1},{1,0},{2,3},{3,2},{4,5},{5,4},{6,7},{7,6},{8,9},{9,8},{10,11... | collective-permute-start | bytes 2949128 | tf_op jit(solution)/shard_map/ppermute | solution.py:27
  136.9 23.0 %collective-permute-start.12 = (f32[384,640]{1,0:T(8,128)S(1)}, f32[384,640]{1,0:T(8,128)S(1)}, u32[]{:S(2)}, u32[]{:S(2)}) collective-permute-start(f32[384,640]{1,0:T(8,128)S(1)} %collective-permute-done.7.refs_11_), channel_id=1, source_target_pairs={{0,2},{1,3},{2,0},{3,1},{4,6},{5,7},{6,4},{7,5},{8,10},{9,11},{10,... | collective-permute-start | bytes 2949128 | tf_op jit(solution)/shard_map/ppermute | solution.py:27
  137.4 46.8 %copy-start.1 = (f32[1,1,512]{2,1,0:T(1,128)S(1)}, f32[1,1,512]{2,1,0:T(1,128)}, u32[]{:S(2)}) copy-start(f32[1,1,512]{2,1,0:T(1,128)} %param.4) | copy-start | bytes 6148
  137.4 46.8 %copy-start.3 = (s32[8,1,12]{2,1,0:T(1,128)S(1)}, s32[8,1,12]{2,1,0:T(1,128)}, u32[]{:S(2)}) copy-start(s32[8,1,12]{2,1,0:T(1,128)} %param.5) | copy-start | bytes 1156
  152.5 1.3 copy-start.4
  153.8 6.1 %collective-permute-start.13 = (f32[384,640]{1,0:T(8,128)S(1)}, f32[384,640]{1,0:T(8,128)S(1)}, u32[]{:S(2)}, u32[]{:S(2)}) collective-permute-start(f32[384,640]{1,0:T(8,128)S(1)} %collective-permute-done.7.refs_11_), channel_id=1, source_target_pairs={{0,1},{1,0},{2,3},{3,2},{4,5},{5,4},{6,7},{7,6},{8,9},{9,8},{10,11... | collective-permute-start | bytes 2949128 | tf_op jit(solution)/shard_map/ppermute | solution.py:27
  153.8 29.1 %collective-permute-start.11 = (f32[384,640]{1,0:T(8,128)S(1)}, f32[384,640]{1,0:T(8,128)S(1)}, u32[]{:S(2)}, u32[]{:S(2)}) collective-permute-start(f32[384,640]{1,0:T(8,128)S(1)} %collective-permute-done.9.refs_8_), channel_id=1, source_target_pairs={{0,1},{1,0},{2,3},{3,2},{4,5},{5,4},{6,7},{7,6},{8,9},{9,8},{10,11... | collective-permute-start | bytes 2949128 | tf_op jit(solution)/shard_map/ppermute | solution.py:27
  159.9 23.0 %collective-permute-start.14 = (f32[384,640]{1,0:T(8,128)S(1)}, f32[384,640]{1,0:T(8,128)S(1)}, u32[]{:S(2)}, u32[]{:S(2)}) collective-permute-start(f32[384,640]{1,0:T(8,128)S(1)} %collective-permute-done.12.refs_12_), channel_id=1, source_target_pairs={{0,1},{1,0},{2,3},{3,2},{4,5},{5,4},{6,7},{7,6},{8,9},{9,8},{10,11... | collective-permute-start | bytes 2949128 | tf_op jit(solution)/shard_map/ppermute | solution.py:27
  182.9 1.4 copy-start.5

commit v2 on v1

--- a/solution.py
+++ b/solution.py
@@ -209,35 +209,59 @@
     lax.fori_loop(first, last, step, 0)
 
 
-def parent_kernel(*refs, count, skip, width, devices):
-    pieces = 2 * devices
-    table, heads, weights, slab, inverse, fronts_here, far = refs[:7]
-    edges = refs[7 : 7 + pieces]
-    leaf_out, panel_out, update_out = refs[7 + pieces : 10 + pieces]
-    (
-        edge, here, beyond, leaf_panel, own_panel, panel_high, panel_low, column,
-        two_left, two_right, total, a, edge_done, rows_done, out_done,
-    ) = refs[10 + pieces :]
+def at(tile):
+    return pl.ds(pl.multiple_of(tile * TILE, TILE), TILE)
+
+
+def goal_of(table, i, tile):
+    entry = 3 * (tile >> 2) + (tile & 3) - 1
+    return jnp.where((tile & 3) == 0, -1, table[place()[0] ^ i, jnp.maximum(entry, 0)])
+
+
+def panel_of(inverse):
+    turned = halves(inverse)
+    cut = inverse.shape[0] // 2
+    top = tuple(part[:cut, :cut] for part in turned)
+    bottom = tuple(part[cut:, :] for part in turned)
+
+    def product(block):
+        full = halves(block)
+        left = split_dot(tuple(part[:, :cut] for part in full), top)
+        return jnp.concatenate([left, split_dot(full, bottom)], axis=1)
+
+    return product
+
+
+def add_columns(table, i, edge, panel_high, panel_low, column, *, count, skip, devices):
+    front = place()[1]
+    separator = panel_high.shape[2]
+    first = slice((1 - skip) * TILE, (2 - skip) * TILE)
+    slot = slot_of(front, devices)
+    one = panel_high[slot, first, :], panel_low[slot, first, :]
+    for s in range(devices):
+        piece = edge[s, :, separator:] - split_dot((panel_high[s], panel_low[s]), one)
+        owner = front ^ offset_of(s, devices)
+        for t in range(count - skip):
+            target = goal_of(table, i, owner * count + skip + t)
+
+            @pl.when(target >= 0)
+            def _():
+                column[at(target), :] += piece[t * TILE : (t + 1) * TILE, :]
+
+
+def own_kernel(*refs, count, skip, width, devices):
+    table, heads, weights, slab, inverse, fronts_here = refs[:6]
+    edges = refs[6 : 6 + devices]
+    leaf_panel, column, total_out = refs[6 + devices : 9 + devices]
+    edge, here, panel_high, panel_low, total, edge_done, done = refs[9 + devices :]
     leaf, front, half = place()
     sent = count - skip
     separator = width // GROUP_TILES
     rows = count * TILE
-    first_row = pl.multiple_of((front * 2 + half) * rows, TILE)
-
-    def at(tile):
-        return pl.ds(pl.multiple_of(tile * TILE, TILE), TILE)
-
-    def goal_of(i, tile):
-        entry = 3 * (tile >> 2) + (tile & 3) - 1
-        return jnp.where((tile & 3) == 0, -1, table[leaf ^ i, jnp.maximum(entry, 0)])
-
-    copies = [
-        pltpu.make_async_copy(edges[k], edge.at[k // devices, k % devices], edge_done.at[k]) for k in range(pieces)
-    ]
-    copies += [
-        pltpu.make_async_copy(fronts_here.at[skip * TILE :, :], here, rows_done.at[0]),
-        pltpu.make_async_copy(far, beyond, rows_done.at[1]),
-    ]
+    first_row = (front * 2 + half) * rows
+
+    copies = [pltpu.make_async_copy(edges[s], edge.at[s], edge_done.at[s]) for s in range(devices)]
+    copies.append(pltpu.make_async_copy(fronts_here.at[skip * TILE :, :], here, done.at[0]))
     for copy in copies:
         copy.start()
 
@@ -268,70 +292,67 @@
         def _():
             total[line, at(mine + 1)] = -behind
 
-    leaf_copy = pltpu.make_async_copy(leaf_panel, leaf_out, out_done.at[0])
-    for i in range(2):
-        turned = halves(inverse[i])
-        cut = separator // 2
-        top = tuple(part[:cut, :cut] for part in turned)
-        bottom = tuple(part[cut:, :] for part in turned)
-
-        def panel_of(block):
-            full = halves(block)
-            return jnp.concatenate(
-                [split_dot(tuple(part[:, :cut] for part in full), top), split_dot(full, bottom)], axis=1
-            )
-
-        for s in range(devices):
-            copies[i * devices + s].wait()
-            panel = panel_of(edge[i, s, :, :separator])
-            if s == 0 and i == 0:
-                leaf_panel[skip * TILE :, :] = panel
-                if skip:
-                    leaf_panel[:TILE, :] = panel_of(slab[:TILE, :])
-                leaf_copy.start()
-            panel_high[i, s], panel_low[i, s] = halves(panel)
-
-    tile_one = slice((1 - skip) * TILE, (2 - skip) * TILE)
-    slot = slot_of(front, devices)
-    for i in range(2):
-        one = panel_high[i, slot, tile_one, :], panel_low[i, slot, tile_one, :]
-        for s in range(devices):
-            piece = edge[i, s, :, separator:] - split_dot((panel_high[i, s], panel_low[i, s]), one)
-            owner = front ^ offset_of(s, devices)
-            for t in range(sent):
-                target = goal_of(i, owner * count + skip + t)
-
-                @pl.when(target >= 0)
-                def _():
-                    column[at(target), :] += piece[t * TILE : (t + 1) * TILE, :]
-
-    copies[-2].wait()
+    panel_from = panel_of(inverse[0])
+    if skip:
+        leaf_panel[:TILE, :] = panel_from(slab[:TILE, :])
+    for s in range(devices):
+        copies[s].wait()
+        panel = panel_from(edge[s, :, :separator])
+        if s == 0:
+            leaf_panel[skip * TILE :, :] = panel
+        panel_high[s], panel_low[s] = halves(panel)
+    add_columns(table, 0, edge, panel_high, panel_low, column, count=count, skip=skip, devices=devices)
+
     copies[-1].wait()
-
-    def contribution(i, s):
-        product = split_dot((panel_high[i, 0], panel_low[i, 0]), (panel_high[i, s], panel_low[i, s]))
+    for s in range(devices):
+        product = split_dot((panel_high[0], panel_low[0]), (panel_high[s], panel_low[s]))
         for c in range(sent):
             tile = (front ^ offset_of(s, devices)) * count + skip + c
-            goal = jnp.maximum(goal_of(i, tile), 0)
+            goal = jnp.maximum(goal_of(table, 0, tile), 0)
             for t in range(sent):
-                target = goal_of(i, front * count + skip + t) - (front * 2 + half) * count
+                target = goal_of(table, 0, front * count + skip + t) - (front * 2 + half) * count
                 target = jnp.where((target >= 0) & (target < count), target, count)
                 line = slice(t * TILE, (t + 1) * TILE)
-                if i == 0:
-                    source = here[line, at(tile)]
-                else:
-                    source = beyond[line, at(jnp.maximum(tile - (tile >> 2) - 2, 0))]
-                total[at(target), at(goal)] += source - product[line, c * TILE : (c + 1) * TILE]
-
-    work = [functools.partial(contribution, i, s) for i in range(2) for s in range(devices)]
+                total[at(target), at(goal)] += here[line, at(tile)] - product[line, c * TILE : (c + 1) * TILE]
+    send = pltpu.make_async_copy(total.at[:rows, TILE:], total_out, done.at[1])
+    send.start()
+    send.wait()
+
+
+def parent_kernel(*refs, count, skip, width, devices):
+    table, inverse, column_in, total_in = refs[:4]
+    edges = refs[4 : 4 + devices]
+    panel_out, update_out, far_high, far_low = refs[4 + devices : 8 + devices]
+    edge, panel_high, panel_low, column, two_left, two_right, total, a, edge_done, done = refs[8 + devices :]
+    leaf, front, half = place()
+    separator = width // GROUP_TILES
+    rows = count * TILE
+    first_row = pl.multiple_of((front * 2 + half) * rows, TILE)
+
+    copies = [pltpu.make_async_copy(edges[s], edge.at[s], edge_done.at[s]) for s in range(devices)]
+    copies.append(pltpu.make_async_copy(column_in, column, done.at[0]))
+    copies.append(pltpu.make_async_copy(total_in, total, done.at[1]))
+    for copy in copies:
+        copy.start()
+
+    panel_from = panel_of(inverse[1])
+    for s in range(devices):
+        copies[s].wait()
+        panel_high[s], panel_low[s] = halves(panel_from(edge[s, :, :separator]))
+    sends = [
+        pltpu.make_async_copy(panel_high, far_high, done.at[2]),
+        pltpu.make_async_copy(panel_low, far_low, done.at[3]),
+    ]
+    for send in sends:
+        send.start()
+    copies[devices].wait()
+    add_columns(table, 1, edge, panel_high, panel_low, column, count=count, skip=skip, devices=devices)
+
     a[...] = column[:TILE, :]
-    steps = TILE // SLAB
-    for k, _ in enumerate(factor_steps(a, 1)):
-        while work and len(work) * steps >= (steps - k) * (2 * devices):
-            work.pop(0)()
-    for task in work:
-        task()
-
+    for _ in factor_steps(a, 1):
+        pass
+    row_ids = lax.broadcasted_iota(jnp.int32, (TILE, TILE), 0)
+    col_ids = lax.broadcasted_iota(jnp.int32, (TILE, TILE), 1)
     turned = halves(jnp.where(row_ids >= col_ids, a[...], 0.0))
     for start in range(0, M2, 1024):
         block = slice(start, start + 1024)
@@ -341,23 +362,79 @@
         two_left[block, :] = jnp.concatenate([high, high, low], axis=1)
         two_right[block, :] = jnp.concatenate([high, low, high], axis=1)
     mine = pl.ds(first_row, rows)
-    own_panel[...] = column[mine, :]
-    panel_copy = pltpu.make_async_copy(own_panel, panel_out, out_done.at[1])
-    panel_copy.start()
+    panel_out[...] = column[mine, :]
     own = two_left[mine, :]
-    sends = [leaf_copy, panel_copy]
+    copies[-1].wait()
     for start in range(TILE, M2, 512):
         stop = min(start + 512, M2)
-        total[:rows, start:stop] = total[:rows, start:stop] - plain_dot(own, two_right[start:stop, :])
-        send = pltpu.make_async_copy(
-            total.at[:rows, start:stop],
-            update_out.at[:, start - TILE : stop - TILE],
-            out_done.at[len(sends)],
-        )
+        here = slice(start - TILE, stop - TILE)
+        total[:, here] = total[:, here] - plain_dot(own, two_right[start:stop, :])
+        send = pltpu.make_async_copy(total.at[:, here], update_out.at[:, here], done.at[2 + len(sends)])
         send.start()
         sends.append(send)
     for send in sends:
         send.wait()
+
+
+def far_kernel(table, high, low, far, update, out, panel_high, panel_low, beyond, tiles, loaded, got, put, *, count, skip, devices):
+    leaf, front, half = place()
+    sent = count - skip
+    loads = [
+        pltpu.make_async_copy(high, panel_high, loaded.at[0]),
+        pltpu.make_async_copy(low, panel_low, loaded.at[1]),
+        pltpu.make_async_copy(far, beyond, loaded.at[2]),
+    ]
+    for load in loads:
+        load.start()
+
+    def each(s, t, c):
+        tile = (front ^ offset_of(s, devices)) * count + skip + c
+        goal = goal_of(table, 1, tile)
+        target = goal_of(table, 1, front * count + skip + t) - (front * 2 + half) * count
+        valid = (goal > 0) & (target >= 0) & (target < count)
+        index = (s * sent + t) * sent + c
+        lies = out.at[at(jnp.clip(target, 0, count - 1)), at(jnp.maximum(goal - 1, 0))]
+        return tile, index, valid, lies
+
+    def fetch(index, lies):
+        return pltpu.make_async_copy(lies, tiles.at[index], got.at[index])
+
+    def store(index, lies):
+        return pltpu.make_async_copy(tiles.at[index], lies, put.at[index])
+
+    for s in range(devices):
+        for t in range(sent):
+            for c in range(sent):
+                _, index, valid, lies = each(s, t, c)
+
+                @pl.when(valid)
+                def _():
+                    fetch(index, lies).start()
+
+    for load in loads:
+        load.wait()
+    for s in range(devices):
+        product = split_dot((panel_high[0], panel_low[0]), (panel_high[s], panel_low[s]))
+        for t in range(sent):
+            line = slice(t * TILE, (t + 1) * TILE)
+            for c in range(sent):
+                tile, index, valid, lies = each(s, t, c)
+
+                @pl.when(valid)
+                def _():
+                    source = beyond[line, at(jnp.maximum(tile - (tile >> 2) - 2, 0))]
+                    fetch(index, lies).wait()
+                    tiles[index] += source - product[line, c * TILE : (c + 1) * TILE]
+                    store(index, lies).start()
+
+    for s in range(devices):
+        for t in range(sent):
+            for c in range(sent):
+                _, index, valid, lies = each(s, t, c)
+
+                @pl.when(valid)
+                def _():
+                    store(index, lies).wait()
 
 
 def slab_kernel(matrix, weights, slab, done, *, chosen):
@@ -441,7 +518,7 @@
             jax.ShapeDtypeStruct((sent, len(rest) * TILE), f32),
         ),
         in_specs=[anywhere],
-        out_specs=(anywhere, anywhere),
+        out_specs=(vmem, vmem),
         scratch_shapes=[pltpu.SemaphoreType.DMA((2 * tiles,))],
         compiler_params=params,
         cost_estimate=pl.CostEstimate(flops=0, bytes_accessed=2**23, transcendentals=0),
@@ -456,7 +533,7 @@
 
     state = jax.ShapeDtypeStruct((2, separator, separator), f32)
     scratch = pltpu.VMEM((2 * TILE, TILE), f32)
-    cost = pl.CostEstimate(flops=12 * 10**9, bytes_accessed=2**23, transcendentals=0)
+    cost = pl.CostEstimate(flops=3 * 10**9, bytes_accessed=2**22, transcendentals=0)
     middle = separator // TILE // 2
     half_kernel = functools.partial(corner_kernel, order=separator, count=count, devices=devices)
     state_one, state_two, heads = pl.pallas_call(
@@ -484,37 +561,75 @@
     )(after(state_one, far_edge), state_two)
     other_far_edges = [from_front(after(piece, inverse), 1) for piece in far_edges]
 
-    edges = near_edges + other_edges + far_edges + other_far_edges
-    return pl.pallas_call(
-        functools.partial(parent_kernel, count=count, skip=skip, width=width, devices=devices),
+    sizes = dict(count=count, skip=skip, devices=devices)
+    edge_space = pltpu.VMEM((devices,) + edge.shape, f32)
+    panel_space = pltpu.VMEM((devices, sent, separator), bf16)
+    update_shape = jax.ShapeDtypeStruct((rows, M2 - TILE), f32)
+    panel_shape = jax.ShapeDtypeStruct((devices, sent, separator), bf16)
+    large = pltpu.CompilerParams(vmem_limit_bytes=VMEM_BYTES * 3 // 4)
+    leaf_panel, column, total = pl.pallas_call(
+        functools.partial(own_kernel, width=width, **sizes),
         out_shape=(
             jax.ShapeDtypeStruct((rows, separator), f32),
-            jax.ShapeDtypeStruct((rows, TILE), f32),
-            jax.ShapeDtypeStruct((rows, M2 - TILE), f32),
+            jax.ShapeDtypeStruct((M2, TILE), f32),
+            update_shape,
         ),
-        in_specs=[smem, vmem, vmem, vmem, vmem] + [anywhere] * (2 + len(edges)),
-        out_specs=(anywhere, anywhere, anywhere),
+        in_specs=[smem, vmem, vmem, vmem, vmem] + [anywhere] * (1 + devices),
+        out_specs=(vmem, vmem, anywhere),
         scratch_shapes=[
-            pltpu.VMEM((2, devices) + edge.shape, f32),
+            edge_space,
             pltpu.VMEM((sent, width), f32),
-            pltpu.VMEM(far.shape, f32),
-            pltpu.VMEM((rows, separator), f32),
-            pltpu.VMEM((rows, TILE), f32),
-            pltpu.VMEM((2, devices, sent, separator), bf16),
-            pltpu.VMEM((2, devices, sent, separator), bf16),
+            panel_space,
+            panel_space,
+            pltpu.VMEM((rows + TILE, M2), f32),
+            pltpu.SemaphoreType.DMA((devices,)),
+            pltpu.SemaphoreType.DMA((2,)),
+        ],
+        compiler_params=large,
+        cost_estimate=pl.CostEstimate(flops=2 * 10**9, bytes_accessed=2**22, transcendentals=0),
+        name="own",
+    )(table, heads, weights[None], slab, inverse, matrix, *near_edges, *other_edges)
+    parent_panel, update, far_high, far_low = pl.pallas_call(
+        functools.partial(parent_kernel, width=width, **sizes),
+        out_shape=(jax.ShapeDtypeStruct((rows, TILE), f32), update_shape, panel_shape, panel_shape),
+        in_specs=[smem, vmem] + [anywhere] * (2 + devices),
+        out_specs=(vmem, anywhere, anywhere, anywhere),
+        scratch_shapes=[
+            edge_space,
+            panel_space,
+            panel_space,
             pltpu.VMEM((M2, TILE), f32),
             pltpu.VMEM((M2, 3 * TILE), bf16),
             pltpu.VMEM((M2, 3 * TILE), bf16),
-            pltpu.VMEM((rows + TILE, M2), f32),
+            pltpu.VMEM(update_shape.shape, f32),
             pltpu.VMEM((TILE, TILE), f32),
-            pltpu.SemaphoreType.DMA((len(edges),)),
-            pltpu.SemaphoreType.DMA((2,)),
-            pltpu.SemaphoreType.DMA((2 + M2 // 512,)),
+            pltpu.SemaphoreType.DMA((devices,)),
+            pltpu.SemaphoreType.DMA((4 + M2 // 512,)),
         ],
-        compiler_params=pltpu.CompilerParams(vmem_limit_bytes=VMEM_BYTES * 3 // 4),
-        cost_estimate=pl.CostEstimate(flops=15 * 10**9, bytes_accessed=2**25, transcendentals=0),
+        compiler_params=large,
+        cost_estimate=pl.CostEstimate(flops=3 * 10**9, bytes_accessed=2**22, transcendentals=0),
         name="parent",
-    )(table, heads, weights[None], slab, inverse, matrix, far, *edges)
+    )(table, inverse, column, total, *far_edges, *other_far_edges)
+    update = pl.pallas_call(
+        functools.partial(far_kernel, **sizes),
+        out_shape=update_shape,
+        in_specs=[smem] + [anywhere] * 4,
+        out_specs=anywhere,
+        scratch_shapes=[
+            panel_space,
+            panel_space,
+            pltpu.VMEM(far.shape, f32),
+            pltpu.VMEM((devices * (count - skip) ** 2, TILE, TILE), f32),
+            pltpu.SemaphoreType.DMA((3,)),
+            pltpu.SemaphoreType.DMA((devices * (count - skip) ** 2,)),
+            pltpu.SemaphoreType.DMA((devices * (count - skip) ** 2,)),
+        ],
+        input_output_aliases={4: 0},
+        compiler_params=large,
+        cost_estimate=pl.CostEstimate(flops=10**9, bytes_accessed=2**21, transcendentals=0),
+        name="far",
+    )(table, far_high, far_low, far, update)
+    return leaf_panel, parent_panel, update
 
 
 def on_device(leaf_fronts, screen_weights, parent_tile_index):

time: 216 us -> 134 us (0.62)
  Pallas kernels: 160 us -> 93.9 us
  waiting for transfers between devices: 42.5 us -> 24.9 us
    pallas_call x1, Pallas kernels: 96.7 us -> 3.97 us  [one_front(): pl.pallas_call(functools.partial(body_kernel, skip=skip, chosen=corner +...]
    ppermute x3, waiting for transfers between devices: 30.2 us -> 2.89 us  [from_sibling(): return lax.ppermute(value, 'leaf', pairs)]
    pallas_call x1 -> x3, Pallas kernels: 31.3 us -> 57.6 us  [the longest x1 30 us: one_front(): pl.pallas_call(functools.partial(own_kernel, width=width, **sizes), out_s...]
    ppermute x12, waiting for transfers between devices: 12.3 us -> 22 us  [from_front(): return lax.ppermute(value, 'front', pairs)]
  transfers between devices with their start and end apart: 15 -> 15, of which waited for: 4 -> 6; matrix products, arithmetic and copies ran while one was open for 0% -> 0% of each run, Pallas kernels for 59% -> 64%
where the time goes in v2:
time: 134 us; the launch traced here: 133 us
  Pallas kernels  93.9 us (70%)
  waiting for transfers between devices  24.9 us (19%)
  starting transfers between devices  11.4 us (9%)
    pallas_call x1, Pallas kernels, one_front(): pl.pallas_call(functools.partial(own_kernel, width=width, **sizes), out_s...  30 us
    ppermute x12, waiting for transfers between devices, from_front(): return lax.ppermute(value, 'front', pairs)  22 us
    pallas_call x1, Pallas kernels, one_front(): pl.pallas_call(functools.partial(parent_kernel, width=width, **sizes), ou...  21.2 us
    pallas_call x1, Pallas kernels, one_front(): pl.pallas_call(functools.partial(half_kernel, first=middle, last=separato...  15.1 us
    pallas_call x1, Pallas kernels, one_front(): pl.pallas_call(functools.partial(half_kernel, first=0, last=middle), out_...  14.9 us
    pallas_call x1, Pallas kernels, one_front(): pl.pallas_call(functools.partial(far_kernel, **sizes), out_shape=update_s...  6.49 us
    ppermute x12, starting transfers between devices, from_front(): return lax.ppermute(value, 'front', pairs)  6.17 us
    ppermute x3, starting transfers between devices, from_sibling(): return lax.ppermute(value, 'leaf', pairs)  5.27 us
  transfers between devices with their start and end apart: 15, of which 6 were waited for; matrix products, arithmetic and copies ran while one was open for 0% of the time, Pallas kernels for 64%

profile of v2, /device:TPU:0, one launch (start us, length us, event | category | flops | bytes accessed | tf_op | source)
XLA Modules:
  0.0 132.5 jit_solution(6178839870319794861)
XLA Ops:
  0.6 2.4 %slab.1.refs_0_.refs_3_ = f32[136,512]{1,0:T(8,128)} custom-call(f32[512,2048]{1,0:T(8,128)} %bitcast.11, f32[1,512]{1,0:T(1,128)} %bitcast.9), custom_call_target="tpu_custom_call" | custom-call | bytes 524288 | tf_op jit(solution)/shard_map/slab/pallas_call | solution.py:502
  3.0 0.0 copy-start.1
  3.0 3.0 %collective-permute-start.3 = (f32[136,512]{1,0:T(8,128)}, f32[136,512]{1,0:T(8,128)S(1)}, u32[]{:S(2)}, u32[]{:S(2)}) collective-permute-start(f32[136,512]{1,0:T(8,128)} %slab.1.refs_0_.refs_3_), channel_id=1, source_target_pairs={{0,4},{4,0},{8,12},{12,8},{16,20},{20,16},{24,28},{28,24},{1,5},{5... | collective-permute-start | bytes 835592 | tf_op jit(solution)/shard_map/ppermute | solution.py:32
  6.0 4.0 %body.1 = (f32[384,640]{1,0:T(8,128)}, f32[384,1408]{1,0:T(8,128)}) custom-call(f32[512,2048]{1,0:T(8,128)} %bitcast.12), custom_call_target="tpu_custom_call" | custom-call | bytes 8388608 | tf_op jit(solution)/shard_map/body/pallas_call | solution.py:514
  10.0 2.9 %collective-permute-done.3.refs_4_ = f32[136,512]{1,0:T(8,128)S(1)} collective-permute-done((f32[136,512]{1,0:T(8,128)}, f32[136,512]{1,0:T(8,128)S(1)}, u32[]{:S(2)}, u32[]{:S(2)}) %collective-permute-start.3) | collective-permute-done | bytes 278560 | tf_op jit(solution)/shard_map/ppermute | solution.py:32
  12.9 1.7 %collective-permute-start.7 = (f32[384,640]{1,0:T(8,128)}, f32[384,640]{1,0:T(8,128)S(1)}, u32[]{:S(2)}, u32[]{:S(2)}) collective-permute-start(f32[384,640]{1,0:T(8,128)} %get-tuple-element.35.refs_6_), channel_id=1, source_target_pairs={{0,4},{4,0},{8,12},{12,8},{16,20},{20,16},{24,28},{28,24},{1,5},{5... | collective-permute-start | bytes 2949128 | tf_op jit(solution)/shard_map/ppermute | solution.py:32
  14.7 1.5 %collective-permute-start = (f32[136,512]{1,0:T(8,128)S(1)}, f32[136,512]{1,0:T(8,128)S(1)}, u32[]{:S(2)}, u32[]{:S(2)}) collective-permute-start(f32[136,512]{1,0:T(8,128)S(1)} %copy-done.1), channel_id=1, source_target_pairs={{0,2},{1,3},{2,0},{3,1},{4,6},{5,7},{6,4},{7,5},{8,10},{9,11},{10,... | collective-permute-start | bytes 835592 | tf_op jit(solution)/shard_map/ppermute | solution.py:27
  16.1 0.5 collective-permute-start.4
  16.7 0.0 collective-permute-start.1
  16.7 0.5 collective-permute-start.5
  17.2 7.1 %collective-permute-done.refs_1_ = f32[136,512]{1,0:T(8,128)S(1)} collective-permute-done((f32[136,512]{1,0:T(8,128)S(1)}, f32[136,512]{1,0:T(8,128)S(1)}, u32[]{:S(2)}, u32[]{:S(2)}) %collective-permute-start) | collective-permute-done | bytes 278560 | tf_op jit(solution)/shard_map/ppermute | solution.py:27
  24.2 0.0 collective-permute-start.2
  24.3 3.6 %collective-permute-done.4.refs_5_ = f32[136,512]{1,0:T(8,128)S(1)} collective-permute-done((f32[136,512]{1,0:T(8,128)S(1)}, f32[136,512]{1,0:T(8,128)S(1)}, u32[]{:S(2)}, u32[]{:S(2)}) %collective-permute-start.4) | collective-permute-done | bytes 278560 | tf_op jit(solution)/shard_map/ppermute | solution.py:27
  27.9 0.0 collective-permute-start.6
  27.9 1.5 %collective-permute-start.8 = (f32[384,640]{1,0:T(8,128)}, f32[384,640]{1,0:T(8,128)S(1)}, u32[]{:S(2)}, u32[]{:S(2)}) collective-permute-start(f32[384,640]{1,0:T(8,128)} %get-tuple-element.35.refs_6_), channel_id=1, source_target_pairs={{0,2},{1,3},{2,0},{3,1},{4,6},{5,7},{6,4},{7,5},{8,10},{9,11},{10,... | collective-permute-start | bytes 2949128 | tf_op jit(solution)/shard_map/ppermute | solution.py:27
  29.4 0.1 collective-permute-done.6.refs_7_
  29.4 14.9 %corner_first.1 = (f32[2,512,512]{2,1,0:T(8,128)S(1)}, f32[2,512,512]{2,1,0:T(8,128)S(1)}, f32[2,8,512]{2,1,0:T(8,128)S(1)}) custom-call(f32[136,512]{1,0:T(8,128)S(1)} %copy-done.1, f32[136,512]{1,0:T(8,128)S(1)} %collective-permute-done.refs_1_, f32[136,512]{1,0:T(8,128)S(1)} %collective-permute-done.1.refs_2_, ...), custom_call_target="tpu_custom_call" | custom-call | flops 3000000000 | bytes 4194304 | tf_op jit(solution)/shard_map/corner_first/pallas_call | solution.py:539
  44.3 0.0 collective-permute-done.7.refs_4_
  44.3 1.6 %collective-permute-start.11 = (f32[384,640]{1,0:T(8,128)S(1)}, f32[384,640]{1,0:T(8,128)S(1)}, u32[]{:S(2)}, u32[]{:S(2)}) collective-permute-start(f32[384,640]{1,0:T(8,128)S(1)} %collective-permute-done.7.refs_4_), channel_id=1, source_target_pairs={{0,2},{1,3},{2,0},{3,1},{4,6},{5,7},{6,4},{7,5},{8,10},{9,11},{10,... | collective-permute-start | bytes 2949128 | tf_op jit(solution)/shard_map/ppermute | solution.py:27
  45.9 0.5 collective-permute-start.14
  46.4 0.0 collective-permute-start.9
  46.4 6.3 %collective-permute-done.8.refs_7_ = f32[384,640]{1,0:T(8,128)S(1)} collective-permute-done((f32[384,640]{1,0:T(8,128)}, f32[384,640]{1,0:T(8,128)S(1)}, u32[]{:S(2)}, u32[]{:S(2)}) %collective-permute-start.8) | collective-permute-done | bytes 983072 | tf_op jit(solution)/shard_map/ppermute | solution.py:27
  52.6 0.0 collective-permute-start.10
  52.6 15.1 %corner_second.1.refs_4_.refs_1_ = f32[2,512,512]{2,1,0:T(8,128)S(1)} custom-call(f32[2,512,512]{2,1,0:T(8,128)S(1)} %get-tuple-element.32.refs_0_, f32[2,512,512]{2,1,0:T(8,128)S(1)} %get-tuple-element.33.refs_1_), custom_call_target="tpu_custom_call" | custom-call | flops 3000000000 | bytes 4194304 | tf_op jit(solution)/shard_map/corner_second/pallas_call | solution.py:552
  67.8 0.6 collective-permute-start.12
  68.3 5.0 %collective-permute-done.11.refs_5_ = f32[384,640]{1,0:T(8,128)S(1)} collective-permute-done((f32[384,640]{1,0:T(8,128)S(1)}, f32[384,640]{1,0:T(8,128)S(1)}, u32[]{:S(2)}, u32[]{:S(2)}) %collective-permute-start.11) | collective-permute-done | bytes 983072 | tf_op jit(solution)/shard_map/ppermute | solution.py:27
  73.4 30.0 %own.1 = (f32[512,512]{1,0:T(8,128)}, f32[4096,128]{1,0:T(8,128)S(1)}, f32[512,3968]{1,0:T(8,128)}) custom-call(s32[8,12]{1,0:T(8,128)S(1)} %bitcast.6, f32[2,8,512]{2,1,0:T(8,128)S(1)} %get-tuple-element.29.refs_1_, f32[1,512]{1,0:T(1,128)S(1)} %bitcast.10, f32[136,512]{1,0:T(8,128)S(1)} %copy-done.1, f32[2,512,512]{2,1,0:T(8,128)S(1)} %corner_second.1.refs_4_.refs_1_, ...), custom_call_target="tpu_custom_call" | custom-call | flops 2000000000 | bytes 4194304 | tf_op jit(solution)/shard_map/own/pallas_call | solution.py:570
  103.3 1.3 copy-done
  104.6 0.0 collective-permute-done.12.refs_6_
  104.6 0.0 collective-permute-done.13.refs_7_
  104.7 21.2 %parent.1 = (f32[512,128]{1,0:T(8,128)}, f32[512,3968]{1,0:T(8,128)}, bf16[4,384,512]{2,1,0:T(8,128)(2,1)S(1)}, bf16[4,384,512]{2,1,0:T(8,128)(2,1)S(1)}) custom-call(s32[8,12]{1,0:T(8,128)S(1)} %bitcast.7, f32[2,512,512]{2,1,0:T(8,128)S(1)} %corner_second.1.refs_4_.refs_1_, f32[4096,128]{1,0:T(8,128)} %copy-done, f32[512,3968]{1,0:T(8,128)} %get-tuple-element.39.refs_3_, ...), custom_call_target="tpu_custom_call" | custom-call | flops 3000000000 | bytes 4194304 | tf_op jit(solution)/shard_map/parent/pallas_call | solution.py:592
  125.8 6.5 %far.1 = f32[512,3968]{1,0:T(8,128)} custom-call(s32[8,12]{1,0:T(8,128)S(1)} %bitcast.8, bf16[4,384,512]{2,1,0:T(8,128)(2,1)S(1)} %get-tuple-element.44.high, bf16[4,384,512]{2,1,0:T(8,128)(2,1)S(1)} %get-tuple-element.45.low, f32[384,1408]{1,0:T(8,128)S(1)} %collective-permute-done.14.far, ...), custom_call_target="tpu_custom_call", output_to_operand_aliasing={{}: (4, {})} | custom-call | flops 1000000000 | bytes 2097152 | tf_op jit(solution)/shard_map/far/pallas_call | solution.py:613
  (15 shorter events, 0.0 us)
Async XLA Ops:
  3.0 11.7 %copy-start.1 = (f32[136,512]{1,0:T(8,128)S(1)}, f32[136,512]{1,0:T(8,128)}, u32[]{:S(2)}) copy-start(f32[136,512]{1,0:T(8,128)} %slab.1.refs_0_.refs_3_) | copy-start | bytes 835588
  3.0 9.9 %collective-permute-start.3 = (f32[136,512]{1,0:T(8,128)}, f32[136,512]{1,0:T(8,128)S(1)}, u32[]{:S(2)}, u32[]{:S(2)}) collective-permute-start(f32[136,512]{1,0:T(8,128)} %slab.1.refs_0_.refs_3_), channel_id=1, source_target_pairs={{0,4},{4,0},{8,12},{12,8},{16,20},{20,16},{24,28},{28,24},{1,5},{5... | collective-permute-start | bytes 835592 | tf_op jit(solution)/shard_map/ppermute | solution.py:32
  12.9 33.5 %copy-start.2 = (f32[384,640]{1,0:T(8,128)S(1)}, f32[384,640]{1,0:T(8,128)}, u32[]{:S(2)}) copy-start(f32[384,640]{1,0:T(8,128)} %get-tuple-element.35.refs_6_) | copy-start | bytes 2949124
  12.9 31.4 %collective-permute-start.7 = (f32[384,640]{1,0:T(8,128)}, f32[384,640]{1,0:T(8,128)S(1)}, u32[]{:S(2)}, u32[]{:S(2)}) collective-permute-start(f32[384,640]{1,0:T(8,128)} %get-tuple-element.35.refs_6_), channel_id=1, source_target_pairs={{0,4},{4,0},{8,12},{12,8},{16,20},{20,16},{24,28},{28,24},{1,5},{5... | collective-permute-start | bytes 2949128 | tf_op jit(solution)/shard_map/ppermute | solution.py:32
  14.7 9.6 %collective-permute-start = (f32[136,512]{1,0:T(8,128)S(1)}, f32[136,512]{1,0:T(8,128)S(1)}, u32[]{:S(2)}, u32[]{:S(2)}) collective-permute-start(f32[136,512]{1,0:T(8,128)S(1)} %copy-done.1), channel_id=1, source_target_pairs={{0,2},{1,3},{2,0},{3,1},{4,6},{5,7},{6,4},{7,5},{8,10},{9,11},{10,... | collective-permute-start | bytes 835592 | tf_op jit(solution)/shard_map/ppermute | solution.py:27
  16.1 11.7 %collective-permute-start.4 = (f32[136,512]{1,0:T(8,128)S(1)}, f32[136,512]{1,0:T(8,128)S(1)}, u32[]{:S(2)}, u32[]{:S(2)}) collective-permute-start(f32[136,512]{1,0:T(8,128)S(1)} %collective-permute-done.3.refs_4_), channel_id=1, source_target_pairs={{0,2},{1,3},{2,0},{3,1},{4,6},{5,7},{6,4},{7,5},{8,10},{9,11},{10,... | collective-permute-start | bytes 835592 | tf_op jit(solution)/shard_map/ppermute | solution.py:27
  16.7 11.2 %collective-permute-start.1 = (f32[136,512]{1,0:T(8,128)S(1)}, f32[136,512]{1,0:T(8,128)S(1)}, u32[]{:S(2)}, u32[]{:S(2)}) collective-permute-start(f32[136,512]{1,0:T(8,128)S(1)} %copy-done.1), channel_id=1, source_target_pairs={{0,1},{1,0},{2,3},{3,2},{4,5},{5,4},{6,7},{7,6},{8,9},{9,8},{10,11... | collective-permute-start | bytes 835592 | tf_op jit(solution)/shard_map/ppermute | solution.py:27
  16.7 12.7 %collective-permute-start.5 = (f32[136,512]{1,0:T(8,128)S(1)}, f32[136,512]{1,0:T(8,128)S(1)}, u32[]{:S(2)}, u32[]{:S(2)}) collective-permute-start(f32[136,512]{1,0:T(8,128)S(1)} %collective-permute-done.3.refs_4_), channel_id=1, source_target_pairs={{0,1},{1,0},{2,3},{3,2},{4,5},{5,4},{6,7},{7,6},{8,9},{9,8},{10,11... | collective-permute-start | bytes 835592 | tf_op jit(solution)/shard_map/ppermute | solution.py:27
  24.2 5.1 %collective-permute-start.2 = (f32[136,512]{1,0:T(8,128)S(1)}, f32[136,512]{1,0:T(8,128)S(1)}, u32[]{:S(2)}, u32[]{:S(2)}) collective-permute-start(f32[136,512]{1,0:T(8,128)S(1)} %collective-permute-done.refs_1_), channel_id=1, source_target_pairs={{0,1},{1,0},{2,3},{3,2},{4,5},{5,4},{6,7},{7,6},{8,9},{9,8},{10,11... | collective-permute-start | bytes 835592 | tf_op jit(solution)/shard_map/ppermute | solution.py:27
  27.9 1.6 %collective-permute-start.6 = (f32[136,512]{1,0:T(8,128)S(1)}, f32[136,512]{1,0:T(8,128)S(1)}, u32[]{:S(2)}, u32[]{:S(2)}) collective-permute-start(f32[136,512]{1,0:T(8,128)S(1)} %collective-permute-done.4.refs_5_), channel_id=1, source_target_pairs={{0,1},{1,0},{2,3},{3,2},{4,5},{5,4},{6,7},{7,6},{8,9},{9,8},{10,11... | collective-permute-start | bytes 835592 | tf_op jit(solution)/shard_map/ppermute | solution.py:27
  27.9 24.8 %collective-permute-start.8 = (f32[384,640]{1,0:T(8,128)}, f32[384,640]{1,0:T(8,128)S(1)}, u32[]{:S(2)}, u32[]{:S(2)}) collective-permute-start(f32[384,640]{1,0:T(8,128)} %get-tuple-element.35.refs_6_), channel_id=1, source_target_pairs={{0,2},{1,3},{2,0},{3,1},{4,6},{5,7},{6,4},{7,5},{8,10},{9,11},{10,... | collective-permute-start | bytes 2949128 | tf_op jit(solution)/shard_map/ppermute | solution.py:27
  44.3 29.0 %collective-permute-start.11 = (f32[384,640]{1,0:T(8,128)S(1)}, f32[384,640]{1,0:T(8,128)S(1)}, u32[]{:S(2)}, u32[]{:S(2)}) collective-permute-start(f32[384,640]{1,0:T(8,128)S(1)} %collective-permute-done.7.refs_4_), channel_id=1, source_target_pairs={{0,2},{1,3},{2,0},{3,1},{4,6},{5,7},{6,4},{7,5},{8,10},{9,11},{10,... | collective-permute-start | bytes 2949128 | tf_op jit(solution)/shard_map/ppermute | solution.py:27
  45.9 79.9 %collective-permute-start.14 = (f32[384,1408]{1,0:T(8,128)}, f32[384,1408]{1,0:T(8,128)S(1)}, u32[]{:S(2)}, u32[]{:S(2)}) collective-permute-start(f32[384,1408]{1,0:T(8,128)} %get-tuple-element.47), channel_id=1, source_target_pairs={{0,4},{4,0},{8,12},{12,8},{16,20},{20,16},{24,28},{28,24},{1,5},{5... | collective-permute-start | bytes 6488072 | tf_op jit(solution)/shard_map/ppermute | solution.py:32
  46.4 27.0 %collective-permute-start.9 = (f32[384,640]{1,0:T(8,128)S(1)}, f32[384,640]{1,0:T(8,128)S(1)}, u32[]{:S(2)}, u32[]{:S(2)}) collective-permute-start(f32[384,640]{1,0:T(8,128)S(1)} %copy-done.2), channel_id=1, source_target_pairs={{0,1},{1,0},{2,3},{3,2},{4,5},{5,4},{6,7},{7,6},{8,9},{9,8},{10,11... | collective-permute-start | bytes 2949128 | tf_op jit(solution)/shard_map/ppermute | solution.py:27
  52.6 20.7 %collective-permute-start.10 = (f32[384,640]{1,0:T(8,128)S(1)}, f32[384,640]{1,0:T(8,128)S(1)}, u32[]{:S(2)}, u32[]{:S(2)}) collective-permute-start(f32[384,640]{1,0:T(8,128)S(1)} %collective-permute-done.8.refs_7_), channel_id=1, source_target_pairs={{0,1},{1,0},{2,3},{3,2},{4,5},{5,4},{6,7},{7,6},{8,9},{9,8},{10,11... | collective-permute-start | bytes 2949128 | tf_op jit(solution)/shard_map/ppermute | solution.py:27
  52.6 20.7 %copy-start.3 = (s32[8,1,12]{2,1,0:T(1,128)S(1)}, s32[8,1,12]{2,1,0:T(1,128)}, u32[]{:S(2)}) copy-start(s32[8,1,12]{2,1,0:T(1,128)} %param.5) | copy-start | bytes 1156
  52.6 20.7 %copy-start.4 = (f32[1,1,512]{2,1,0:T(1,128)S(1)}, f32[1,1,512]{2,1,0:T(1,128)}, u32[]{:S(2)}) copy-start(f32[1,1,512]{2,1,0:T(1,128)} %param.4) | copy-start | bytes 6148
  67.8 36.9 %collective-permute-start.12 = (f32[384,640]{1,0:T(8,128)S(1)}, f32[384,640]{1,0:T(8,128)S(1)}, u32[]{:S(2)}, u32[]{:S(2)}) collective-permute-start(f32[384,640]{1,0:T(8,128)S(1)} %collective-permute-done.7.refs_4_), channel_id=1, source_target_pairs={{0,1},{1,0},{2,3},{3,2},{4,5},{5,4},{6,7},{7,6},{8,9},{9,8},{10,11... | collective-permute-start | bytes 2949128 | tf_op jit(solution)/shard_map/ppermute | solution.py:27
  73.3 31.3 %collective-permute-start.13 = (f32[384,640]{1,0:T(8,128)S(1)}, f32[384,640]{1,0:T(8,128)S(1)}, u32[]{:S(2)}, u32[]{:S(2)}) collective-permute-start(f32[384,640]{1,0:T(8,128)S(1)} %collective-permute-done.11.refs_5_), channel_id=1, source_target_pairs={{0,1},{1,0},{2,3},{3,2},{4,5},{5,4},{6,7},{7,6},{8,9},{9,8},{10,11... | collective-permute-start | bytes 2949128 | tf_op jit(solution)/shard_map/ppermute | solution.py:27
  103.3 1.3 copy-start
